TPU v7x, 32 devices: a whole 2x2x4 slice. The times are simulated.
32 devices in a mesh: section: 2 (over core), dp: 16 (over z, y, x).
Axes of the slice: x: 2, y: 2, z: 4, core: 2. Of those that a mesh axis runs over, the one named last changes fastest.
Arguments:
- patches: bfloat16 [16384, 768], P('dp'), may hold values from -6 to 6
- cotangent: bfloat16 [16384, 768], P('dp'), may hold values from -6 to 6
- codes: int32 [16384], P('dp'), may hold values from 0 to 6287, as said below
- lengths: int32 [32, 4], P('dp'), may hold values from 1 to 256, 512 in all within a row
- codebook: bfloat16 [6288, 768], P('dp'), may hold values from -6 to 6
- qkv_weight: bfloat16 [2, 768, 2304], P('section'), may hold values from -0.21875 to 0.21875
- out_weight: bfloat16 [2, 768, 768], P('section'), may hold values from -0.875 to 0.875
- up_weight: bfloat16 [2, 768, 3072], P('section'), may hold values from -0.21875 to 0.21875
- down_weight: bfloat16 [2, 3072, 768], P('section'), may hold values from -0.109375 to 0.109375
- up_bias: bfloat16 [2, 3072], P('section'), may hold values from -2 to 2
- vectors: bfloat16 [2, 8, 768], P('section'), may hold values from -2 to 2
Outputs:
- block_outputs: bfloat16 [2, 16384, 768], P('section', 'dp')
- input_grads: float32 [2, 16384, 768], P('section', 'dp')
- qkv_grad: float32 [2, 768, 2304], P('section', 'dp')
- out_grad: float32 [2, 768, 768], P('section', 'dp')
- up_grad: float32 [2, 768, 3072], P('section', 'dp')
- down_grad: float32 [2, 3072, 768], P('section', 'dp')
- up_bias_grad: float32 [2, 3072], P('section', 'dp')
- vectors_grad: float32 [2, 8, 768], P('section', None, 'dp')
- histogram: int32 [6288], replicated
- code_stats: float32 [2], replicated
Inputs may be any that keep to these rules, and one draw needn't show every extreme that they name: A code's row lives on the index code // 393 of dp. The 1024 codes of one index of dp hold at most 128 codes for any one holding index, and in every draw some holding index gets exactly 128 from every index. `lengths`: each row sums to 512; its largest entry is exactly 256.
All inputs are finite; a program needn't handle non-finite values.
Results may differ from a plain program's by a relative error of at most 0.008.
Values may be sent and summed in bfloat16 or wider, within the bound.
A program may use at most 384 MiB of HBM per device.

v0:
```python
import jax
import jax.numpy as jnp
from jax import lax
from jax.sharding import PartitionSpec as P

HEADS = 12


def shifted(block, axis, distance):
    devices = range(lax.axis_size(axis))
    route = [(i - distance, i) for i in devices if i - distance in devices]
    return lax.ppermute(block, axis, route)


def layer_norm(input_rows, gain_row, bias_row):
    row_mean = jnp.mean(input_rows, axis=-1, keepdims=True)
    centered = input_rows - row_mean
    variance = jnp.mean(centered * centered, axis=-1, keepdims=True)
    return centered * lax.rsqrt(variance + 1e-06) * gain_row + bias_row


def segment_mask(length_row, row_count):
    image_ends = jnp.cumsum(length_row)
    positions = jnp.arange(row_count, dtype=jnp.int32)
    image_label = jnp.sum((positions[:, None] >= image_ends[None, :-1]).astype(jnp.int32), axis=1)
    return image_label[:, None] == image_label[None, :]


def times_transposed(first_term, second_term):
    return lax.dot_general(
        first_term, second_term, (((1,), (1,)), ((), ())), preferred_element_type=jnp.float32
    )


def transposed_times(first_term, second_term):
    return lax.dot_general(
        first_term, second_term, (((0,), (0,)), ((), ())), preferred_element_type=jnp.float32
    )


def pack_grads(gradients, split_dims, devices):
    pieces = []
    for grad_array, split_axis in zip(gradients, split_dims):
        moved = jnp.moveaxis(grad_array, split_axis, 0)
        pieces.append(moved.reshape(devices, -1))
    return jnp.concatenate(pieces, axis=1)


def unpack_grads(packed_row, templates, split_dims, devices):
    results = []
    offset = 0
    flat_row = packed_row.reshape(-1)
    for template, split_axis in zip(templates, split_dims):
        moved_shape = [template.shape[split_axis] // devices] + [
            extent for axis_number, extent in enumerate(template.shape) if axis_number != split_axis
        ]
        count = 1
        for extent in moved_shape:
            count = count * extent
        piece = flat_row[offset : offset + count].reshape(moved_shape)
        results.append(jnp.moveaxis(piece, 0, split_axis))
        offset = offset + count
    return tuple(results)


def forward(parameters, input_rows, allowed):
    qkv_matrix, out_matrix, up_matrix, down_matrix, up_shift, vector_rows = parameters
    row_count, model_width = input_rows.shape
    head_size = model_width // HEADS
    score_scale = head_size ** (-0.5)
    normed = layer_norm(input_rows, 1.0 + vector_rows[0], vector_rows[1]).astype(jnp.bfloat16)
    projected = jnp.dot(normed, qkv_matrix, preferred_element_type=jnp.float32)
    query_rows = (
        (projected[:, :model_width] + vector_rows[2])
        .astype(jnp.bfloat16)
        .reshape(row_count, HEADS, head_size)
    )
    key_rows = (
        projected[:, model_width : 2 * model_width]
        .astype(jnp.bfloat16)
        .reshape(row_count, HEADS, head_size)
    )
    value_rows = (
        (projected[:, 2 * model_width :] + vector_rows[3])
        .astype(jnp.bfloat16)
        .reshape(row_count, HEADS, head_size)
    )
    scores = (
        jnp.einsum("qhd,khd->hqk", query_rows, key_rows, preferred_element_type=jnp.float32)
        * score_scale
    )
    scores = jnp.where(allowed[None], scores, -1e30)
    row_max = jnp.max(scores, axis=-1, keepdims=True)
    exponent = jnp.exp(scores - row_max)
    row_total = jnp.sum(exponent, axis=-1, keepdims=True)
    probabilities = (exponent / row_total).astype(jnp.bfloat16)
    log_total = row_max + jnp.log(row_total)
    mixed_heads = jnp.einsum(
        "hqk,khd->qhd", probabilities, value_rows, preferred_element_type=jnp.float32
    )
    mixed_heads = mixed_heads.reshape(row_count, model_width).astype(jnp.bfloat16)
    hidden = (
        input_rows
        + jnp.dot(mixed_heads, out_matrix, preferred_element_type=jnp.float32)
        + vector_rows[4]
    )
    normed_two = layer_norm(hidden, 1.0 + vector_rows[5], vector_rows[6]).astype(jnp.bfloat16)
    pre_act = jnp.dot(normed_two, up_matrix, preferred_element_type=jnp.float32) + up_shift
    activated = jax.nn.gelu(pre_act).astype(jnp.bfloat16)
    block_out = (
        hidden
        + jnp.dot(activated, down_matrix, preferred_element_type=jnp.float32)
        + vector_rows[7]
    )
    kept = (
        input_rows,
        normed,
        query_rows,
        key_rows,
        value_rows,
        log_total,
        mixed_heads,
        hidden,
        normed_two,
        pre_act,
        activated,
    )
    return (block_out, kept)


def backward(parameters, kept, allowed, grad_out):
    qkv_matrix, out_matrix, up_matrix, down_matrix, up_shift, vector_rows = parameters
    (
        input_rows,
        normed,
        query_rows,
        key_rows,
        value_rows,
        log_total,
        mixed_heads,
        hidden,
        normed_two,
        pre_act,
        activated,
    ) = kept
    row_count, model_width = input_rows.shape
    head_size = model_width // HEADS
    score_scale = head_size ** (-0.5)
    grad_branch = grad_out.astype(jnp.bfloat16)
    grad_down_bias = jnp.sum(grad_branch.astype(jnp.float32), axis=0)
    grad_down = transposed_times(activated, grad_branch)
    grad_activated = times_transposed(grad_branch, down_matrix)
    gelu_value, gelu_back = jax.vjp(jax.nn.gelu, pre_act)
    grad_pre = gelu_back(grad_activated)[0].astype(jnp.bfloat16)
    grad_up_bias = jnp.sum(grad_pre.astype(jnp.float32), axis=0)
    grad_up = transposed_times(normed_two, grad_pre)
    grad_normed_two = times_transposed(grad_pre, up_matrix)
    norm_value, norm_back = jax.vjp(layer_norm, hidden, 1.0 + vector_rows[5], vector_rows[6])
    grad_hidden_part, grad_gain_two, grad_shift_two = norm_back(grad_normed_two)
    grad_hidden = grad_out + grad_hidden_part
    grad_attn = grad_hidden.astype(jnp.bfloat16)
    grad_out_bias = jnp.sum(grad_attn.astype(jnp.float32), axis=0)
    grad_out_matrix = transposed_times(mixed_heads, grad_attn)
    grad_mixed = (
        times_transposed(grad_attn, out_matrix)
        .astype(jnp.bfloat16)
        .reshape(row_count, HEADS, head_size)
    )
    scores = (
        jnp.einsum("qhd,khd->hqk", query_rows, key_rows, preferred_element_type=jnp.float32)
        * score_scale
    )
    scores = jnp.where(allowed[None], scores, -1e30)
    exact_probs = jnp.exp(scores - log_total)
    probabilities = exact_probs.astype(jnp.bfloat16)
    grad_probs = jnp.einsum(
        "qhd,khd->hqk", grad_mixed, value_rows, preferred_element_type=jnp.float32
    )
    grad_value = jnp.einsum(
        "hqk,qhd->khd", probabilities, grad_mixed, preferred_element_type=jnp.float32
    ).astype(jnp.bfloat16)
    grad_scores = exact_probs * (
        grad_probs - jnp.sum(grad_probs * exact_probs, axis=-1, keepdims=True)
    )
    grad_scores = grad_scores.astype(jnp.bfloat16)
    grad_query = (
        jnp.einsum("hqk,khd->qhd", grad_scores, key_rows, preferred_element_type=jnp.float32)
        * score_scale
    ).astype(jnp.bfloat16)
    grad_key = (
        jnp.einsum("hqk,qhd->khd", grad_scores, query_rows, preferred_element_type=jnp.float32)
        * score_scale
    ).astype(jnp.bfloat16)
    grad_query = grad_query.reshape(row_count, model_width)
    grad_key = grad_key.reshape(row_count, model_width)
    grad_value = grad_value.reshape(row_count, model_width)
    grad_projected = jnp.concatenate([grad_query, grad_key, grad_value], axis=1)
    grad_qkv = transposed_times(normed, grad_projected)
    grad_normed = times_transposed(grad_projected, qkv_matrix)
    first_value, first_back = jax.vjp(layer_norm, input_rows, 1.0 + vector_rows[0], vector_rows[1])
    grad_input_part, grad_gain_one, grad_shift_one = first_back(grad_normed)
    grad_input = grad_hidden + grad_input_part
    grad_vectors = jnp.stack(
        [
            grad_gain_one,
            grad_shift_one,
            jnp.sum(grad_query.astype(jnp.float32), axis=0),
            jnp.sum(grad_value.astype(jnp.float32), axis=0),
            grad_out_bias,
            grad_gain_two,
            grad_shift_two,
            grad_down_bias,
        ]
    )
    return ((grad_qkv, grad_out_matrix, grad_up, grad_down, grad_up_bias, grad_vectors), grad_input)


def add_pair(first_term, second_term):
    return first_term + second_term


def body(
    patches,
    cotangent,
    codes,
    lengths,
    codebook,
    qkv_weight,
    out_weight,
    up_weight,
    down_weight,
    up_bias,
    vectors,
):
    parameters = (
        qkv_weight[0],
        out_weight[0],
        up_weight[0],
        down_weight[0],
        up_bias[0].astype(jnp.float32),
        vectors[0].astype(jnp.float32),
    )
    section_index = lax.axis_index("section")
    is_first = section_index == 0
    devices = lax.axis_size("dp")
    tok_rows, model_width = patches.shape
    shard_rows = codebook.shape[0]
    micro_count = lengths.shape[0]
    row_count = tok_rows // micro_count
    codebook_all = lax.all_gather(codebook, "dp", axis=0, tiled=True)
    chosen = jnp.take(codebook_all, codes, axis=0)
    local_counts = jnp.zeros((shard_rows * devices,), jnp.int32).at[codes].add(1)
    histogram = lax.psum(local_counts, "dp")
    code_share = histogram.astype(jnp.float32) / (tok_rows * devices)
    is_used = histogram > 0
    usage_share = jnp.mean(is_used.astype(jnp.float32))
    entropy = -jnp.sum(
        jnp.where(is_used, code_share * jnp.log(jnp.where(is_used, code_share, 1.0)), 0.0)
    )
    code_stats = jnp.stack([usage_share, jnp.exp(entropy) / histogram.shape[0]])
    split_dims = (0, 0, 0, 0, 0, 1)
    full_zeros = tuple((jnp.zeros(weight_array.shape, jnp.float32) for weight_array in parameters))
    grad_sums = full_zeros

    def one_turn(turn_index, loop_state):
        outputs, input_grad, received, grad_sums = loop_state
        micro_index = turn_index - 1 + section_index
        is_valid = jnp.logical_and(micro_index >= 0, micro_index < micro_count)
        clipped = jnp.clip(micro_index, 0, micro_count - 1)
        row_start = clipped * row_count
        patch_rows = lax.dynamic_slice_in_dim(patches, row_start, row_count, 0)
        code_rows = lax.dynamic_slice_in_dim(chosen, row_start, row_count, 0)
        cot_rows = lax.dynamic_slice_in_dim(cotangent, row_start, row_count, 0)
        length_row = lax.dynamic_index_in_dim(lengths, clipped, 0, keepdims=False)
        allowed = segment_mask(length_row, row_count)

        def work(operands):
            patch_rows, code_rows, cot_rows, received, allowed = operands
            input_rows = jnp.where(is_first, patch_rows, code_rows).astype(jnp.float32)
            block_out, kept = forward(parameters, input_rows, allowed)
            grad_out = jnp.where(
                is_first,
                received.astype(jnp.float32) + 0.5 * (block_out - code_rows.astype(jnp.float32)),
                cot_rows.astype(jnp.float32),
            )
            gradients, grad_input = backward(parameters, kept, allowed, grad_out)
            grad_input = jnp.where(
                is_first, grad_input, grad_input.astype(jnp.bfloat16).astype(jnp.float32)
            )
            return (block_out.astype(jnp.bfloat16), grad_input, gradients)

        def resting(operands):
            return (
                jnp.zeros((row_count, model_width), jnp.bfloat16),
                jnp.zeros((row_count, model_width), jnp.float32),
                full_zeros,
            )

        block_out, grad_input, gradients = lax.cond(
            is_valid, work, resting, (patch_rows, code_rows, cot_rows, received, allowed)
        )
        old_out = lax.dynamic_slice_in_dim(outputs, row_start, row_count, 0)
        outputs = lax.dynamic_update_slice_in_dim(
            outputs, jnp.where(is_valid, block_out, old_out), row_start, 0
        )
        old_grad = lax.dynamic_slice_in_dim(input_grad, row_start, row_count, 0)
        input_grad = lax.dynamic_update_slice_in_dim(
            input_grad, jnp.where(is_valid, grad_input, old_grad), row_start, 0
        )
        received = shifted(grad_input.astype(jnp.bfloat16), "section", -1)
        grad_sums = jax.tree.map(add_pair, grad_sums, gradients)
        return (outputs, input_grad, received, grad_sums)

    start_state = (
        jnp.zeros((tok_rows, model_width), jnp.bfloat16),
        jnp.zeros((tok_rows, model_width), jnp.float32),
        jnp.zeros((row_count, model_width), jnp.bfloat16),
        grad_sums,
    )
    outputs, input_grad, received, grad_sums = lax.fori_loop(
        0, micro_count + 1, one_turn, start_state
    )
    packed = pack_grads(grad_sums, split_dims, devices)
    summed_row = lax.psum_scatter(packed, "dp", scatter_dimension=0, tiled=True)
    weight_grads = unpack_grads(summed_row, parameters, split_dims, devices)
    return (
        outputs[None],
        input_grad[None],
        weight_grads[0][None],
        weight_grads[1][None],
        weight_grads[2][None],
        weight_grads[3][None],
        weight_grads[4][None],
        weight_grads[5][None],
        histogram,
        code_stats,
    )


def solution(mesh):
    placed = (
        P("dp", None),
        P("dp", None),
        P("dp"),
        P("dp", None),
        P("dp", None),
        P("section", None, None),
        P("section", None, None),
        P("section", None, None),
        P("section", None, None),
        P("section", None),
        P("section", None, None),
    )
    return jax.shard_map(
        body,
        mesh=mesh,
        in_specs=placed,
        out_specs=(
            P("section", "dp", None),
            P("section", "dp", None),
            P("section", "dp", None),
            P("section", "dp", None),
            P("section", "dp", None),
            P("section", "dp", None),
            P("section", "dp"),
            P("section", None, "dp"),
            P(),
            P(),
        ),
        check_vma=False,
    )
```

profile of v0, /device:TPU:0, one launch (start us, length us, event | category | flops | bytes accessed | tf_op | source)
XLA Modules:
  0.0 1453.6 jit_solution(8758084817118383273)
XLA Ops:
  12.6 126.9 %all-gather.3.cloned.1.call-done = bf16[16,393,768]{2,1,0:T(8,128)(2,1)} async-done(((bf16[1,393,768]{2,1,0:T(8,128)(2,1)}), bf16[16,393,768]{2,1,0:T(8,128)(2,1)}) %all-gather.3.cloned.1.call-update) | async-done | bytes 9658384 | tf_op jit(solution)/shard_map/all_gather | solution.py:250
  139.6 12.1 reshape.236
  151.6 9.5 gather_fusion
  166.6 467.3 %while.32 = (s32[]{:T(128)}, bf16[1024,768]{1,0:T(8,128)(2,1)}, f32[1024,768]{1,0:T(8,128)}, bf16[512,768]{1,0:T(8,128)(2,1)}, f32[768,2304]{1,0:T(8,128)}, /*in...) while((s32[]{:T(128)}, bf16[1024,768]{1,0:T(8,128)(2,1)}, ...), condition=%wide.region_25.26_spmd.clone, body=%wide.region_0.25_spmd.clone.sunk | while | flops 24387528704 | bytes 695229952 | solution.py:320
  167.8 21.1 %conditional.3 = (bf16[512,768]{1,0:T(8,128)(2,1)}, f32[512,768]{1,0:T(8,128)}, f32[768,2304]{1,0:T(8,128)}, f32[768,768]{1,0:T(8,128)}, f32[768,3072]{1,0:T(8,1...) conditional(s32[]{:T(128)} %convert_element_type.318, () %tuple.97, (pred[]{:T(512)}, ...), branch_computations={%region_2.2_spmd, %region_3.24_spmd} | conditional | flops 24372170752 | bytes 567415168 | solution.py:299
  167.8 4.8 broadcast_in_dim.118
  172.6 4.3 broadcast_in_dim.119
  194.0 10.3 select_add_fusion.14
  204.3 8.5 select_add_fusion.15
  212.8 6.9 select_add_fusion.12
  224.2 70.1 %collective-permute-done = bf16[512,768]{1,0:T(8,128)(2,1)} collective-permute-done((bf16[512,768]{1,0:T(8,128)(2,1)S(1)}, bf16[512,768]{1,0:T(8,128)(2,1)}, u32[]{:S(2)}, u32[]{:S(2)}) %collective-permute-start) | collective-permute-done | bytes 786464 | tf_op jit(solution)/shard_map/while/body/eval_jaxpr/ppermute | solution.py:12
  295.3 120.2 %conditional.3 = (bf16[512,768]{1,0:T(8,128)(2,1)}, f32[512,768]{1,0:T(8,128)}, f32[768,2304]{1,0:T(8,128)}, f32[768,768]{1,0:T(8,128)}, f32[768,3072]{1,0:T(8,1...) conditional(s32[]{:T(128)} %convert_element_type.318, () %tuple.97, (pred[]{:T(512)}, ...), branch_computations={%region_2.2_spmd, %region_3.24_spmd} | conditional | flops 24372170752 | bytes 567415168 | solution.py:299
  298.7 4.2 fusion.50
  316.6 7.3 fusion.31
  325.2 5.5 fusion.54
  330.8 7.2 convert_reduce_fusion.2
  338.0 6.7 convert_reduce_fusion
  354.3 13.5 multiply_reduce_fusion
  367.8 7.0 multiply_convert_fusion
  386.4 9.0 fusion.53
  395.4 10.4 fusion.39
  405.8 5.2 fusion.32
  420.5 13.0 select_add_fusion.14
  433.6 11.3 select_add_fusion.15
  444.9 8.9 select_add_fusion.12
  460.8 120.2 %conditional.3 = (bf16[512,768]{1,0:T(8,128)(2,1)}, f32[512,768]{1,0:T(8,128)}, f32[768,2304]{1,0:T(8,128)}, f32[768,768]{1,0:T(8,128)}, f32[768,3072]{1,0:T(8,1...) conditional(s32[]{:T(128)} %convert_element_type.318, () %tuple.97, (pred[]{:T(512)}, ...), branch_computations={%region_2.2_spmd, %region_3.24_spmd} | conditional | flops 24372170752 | bytes 567415168 | solution.py:299
  464.2 4.2 fusion.50
  482.1 7.2 fusion.31
  490.7 5.5 fusion.54
  496.3 7.2 convert_reduce_fusion.2
  503.5 6.9 convert_reduce_fusion
  520.0 13.5 multiply_reduce_fusion
  533.5 7.0 multiply_convert_fusion
  552.1 9.0 fusion.53
  561.1 10.4 fusion.39
  571.5 5.2 fusion.32
  586.0 13.0 select_add_fusion.14
  599.1 11.3 select_add_fusion.15
  610.4 8.9 select_add_fusion.12
  633.8 5.5 reshape.208
  639.3 6.4 constant_dynamic-update-slice_fusion.3
  647.4 10.5 reshape.210
  658.0 10.8 reshape.211
  670.9 7.8 constant_dynamic-update-slice_fusion.1
  686.8 6.1 scatter_custom_fusion
  692.9 79.4 %psum.7 = s32[6288]{0:T(1024)S(1)} all-reduce(s32[6288]{0:T(1024)S(1)} %scatter_custom_fusion), channel_id=1, replica_groups=mesh['section'=2,'dp'=16] {'dp'}, use_global_device_ids=true, to_apply=%region_28.29 | all-reduce | flops 6288 | bytes 50304 | tf_op jit(solution)/shard_map/psum | solution.py:253
  775.4 648.2 %all-reduce.3.cloned.1.call-done = f32[16,442944]{1,0:T(8,128)} async-done(((f32[16,442944]{1,0:T(8,128)}), f32[16,442944]{1,0:T(8,128)}) %all-reduce.3.cloned.1.call-update) | async-done | bytes 28348432
  1423.6 9.3 dynamic-slice_reduce_fusion
  (419 shorter events, 165.7 us)
Async XLA Ops:
  7.2 132.4 %all-gather.3.cloned.1.call-start = ((), (), s32[]{:S(2)}) async-start(), calls=%async_computation | async-start | bytes 10444800 | tf_op jit(solution)/shard_map/all_gather | solution.py:250
  7.9 1415.7 %all-reduce.3.cloned.1.call-start = ((), (), s32[]{:S(2)}) async-start(), calls=%async_computation.1 | async-start | bytes 56705024
  192.7 101.7 %collective-permute-start = (bf16[512,768]{1,0:T(8,128)(2,1)S(1)}, bf16[512,768]{1,0:T(8,128)(2,1)}, u32[]{:S(2)}, u32[]{:S(2)}) collective-permute-start(bf16[512,768]{1,0:T(8,128)(2,1)S(1)} %get-tuple-element.990), channel_id=1, source_target_pairs={{16,0},{17,1},{18,2},{19,3},{20,4},{21,5},{22,6},{23,7},{24,8},{25... | collective-permute-start | bytes 2359304 | tf_op jit(solution)/shard_map/while/body/eval_jaxpr/ppermute | solution.py:12
  224.2 70.1 %copy-start.9 = (f32[768,768]{1,0:T(8,128)}, f32[768,768]{1,0:T(8,128)S(1)}, u32[]{:S(2)}) copy-start(f32[768,768]{1,0:T(8,128)S(1)} %select_add_fusion.13) | copy-start | bytes 7077892 | tf_op jit(solution)/shard_map/while
  298.7 26.5 %copy-start.38 = (f32[768]{0:T(1024)}, f32[768]{0:T(1024)S(1)}, u32[]{:S(2)}) copy-start(f32[768]{0:T(1024)S(1)} %get-tuple-element.760) | copy-start | bytes 9220 | tf_op jit(solution)/shard_map/while/body/eval_jaxpr/cond
  298.7 49.6 %copy-start.31 = (f32[768]{0:T(1024)}, f32[768]{0:T(1024)S(1)}, u32[]{:S(2)}) copy-start(f32[768]{0:T(1024)S(1)} %get-tuple-element.758) | copy-start | bytes 9220 | tf_op jit(solution)/shard_map/while/body/eval_jaxpr/cond
  324.8 23.5 %copy-start.5 = (f32[512,768]{1,0:T(8,128)}, f32[512,768]{1,0:T(8,128)S(1)}, u32[]{:S(2)}) copy-start(f32[512,768]{1,0:T(8,128)S(1)} %get-tuple-element.828) | copy-start | bytes 4718596 | tf_op jit(solution)/shard_map/while/body/eval_jaxpr/cond
  325.2 23.1 %copy-start.33 = (f32[512]{0:T(512)}, f32[512]{0:T(512)S(1)}, u32[]{:S(2)}) copy-start(f32[512]{0:T(512)S(1)} %fusion.36) | copy-start | bytes 6148 | tf_op jit(solution)/shard_map/while/body/eval_jaxpr/cond
  330.8 14.0 slice-start.6
  338.0 11.0 copy-start.3
  354.3 13.5 slice-start
  354.3 13.5 slice-start.1
  354.3 13.5 slice-start.2
  386.3 9.0 copy-start.4
  386.3 9.0 copy-start.43
  395.3 10.4 copy-start.17
  395.3 10.4 copy-start.21
  395.4 10.4 copy-start.37
  395.4 10.4 copy-start.48
  419.2 39.0 %collective-permute-start = (bf16[512,768]{1,0:T(8,128)(2,1)S(1)}, bf16[512,768]{1,0:T(8,128)(2,1)}, u32[]{:S(2)}, u32[]{:S(2)}) collective-permute-start(bf16[512,768]{1,0:T(8,128)(2,1)S(1)} %get-tuple-element.990), channel_id=1, source_target_pairs={{16,0},{17,1},{18,2},{19,3},{20,4},{21,5},{22,6},{23,7},{24,8},{25... | collective-permute-start | bytes 2359304 | tf_op jit(solution)/shard_map/while/body/eval_jaxpr/ppermute | solution.py:12
  444.8 8.9 copy-start.25
  444.8 8.9 copy-start.28
  444.8 8.9 copy-start.22
  464.2 26.5 %copy-start.38 = (f32[768]{0:T(1024)}, f32[768]{0:T(1024)S(1)}, u32[]{:S(2)}) copy-start(f32[768]{0:T(1024)S(1)} %get-tuple-element.760) | copy-start | bytes 9220 | tf_op jit(solution)/shard_map/while/body/eval_jaxpr/cond
  464.2 49.8 %copy-start.31 = (f32[768]{0:T(1024)}, f32[768]{0:T(1024)S(1)}, u32[]{:S(2)}) copy-start(f32[768]{0:T(1024)S(1)} %get-tuple-element.758) | copy-start | bytes 9220 | tf_op jit(solution)/shard_map/while/body/eval_jaxpr/cond
  490.3 23.7 %copy-start.5 = (f32[512,768]{1,0:T(8,128)}, f32[512,768]{1,0:T(8,128)S(1)}, u32[]{:S(2)}) copy-start(f32[512,768]{1,0:T(8,128)S(1)} %get-tuple-element.828) | copy-start | bytes 4718596 | tf_op jit(solution)/shard_map/while/body/eval_jaxpr/cond
  490.7 23.4 %copy-start.33 = (f32[512]{0:T(512)}, f32[512]{0:T(512)S(1)}, u32[]{:S(2)}) copy-start(f32[512]{0:T(512)S(1)} %fusion.36) | copy-start | bytes 6148 | tf_op jit(solution)/shard_map/while/body/eval_jaxpr/cond
  496.3 14.2 slice-start.6
  503.5 11.2 copy-start.3
  520.0 13.5 slice-start
  520.0 13.5 slice-start.1
  520.0 13.5 slice-start.2
  552.0 9.0 copy-start.4
  552.0 9.0 copy-start.43
  561.0 10.4 copy-start.17
  561.1 10.4 copy-start.21
  561.1 10.4 copy-start.37
  561.1 10.4 copy-start.48
  584.7 39.0 %collective-permute-start = (bf16[512,768]{1,0:T(8,128)(2,1)S(1)}, bf16[512,768]{1,0:T(8,128)(2,1)}, u32[]{:S(2)}, u32[]{:S(2)}) collective-permute-start(bf16[512,768]{1,0:T(8,128)(2,1)S(1)} %get-tuple-element.990), channel_id=1, source_target_pairs={{16,0},{17,1},{18,2},{19,3},{20,4},{21,5},{22,6},{23,7},{24,8},{25... | collective-permute-start | bytes 2359304 | tf_op jit(solution)/shard_map/while/body/eval_jaxpr/ppermute | solution.py:12
  610.4 8.9 copy-start.28
  610.4 8.9 copy-start.22
  658.0 10.9 copy-start.30
  658.0 10.9 copy-start.27
  658.0 11.3 copy-start.24
  669.3 9.4 slice-start.3
  670.9 9.1 slice-start.5
  686.8 87.5 %copy-start.49 = (u32[32]{0:T(128)S(1)}, u32[32]{0:T(128)}, u32[]{:S(2)}) copy-start(u32[32]{0:T(128)} %constant.204) | copy-start | bytes 388
  772.3 667.1 %copy-start.35 = (s32[6288]{0:T(1024)}, s32[6288]{0:T(1024)S(1)}, u32[]{:S(2)}) copy-start(s32[6288]{0:T(1024)S(1)} %psum.7) | copy-start | bytes 75460
  (80 other events, 349.7 us)
Sparse Core Ops, SparseCore 0:
  10.8 128.7 all-gather.2
  686.9 736.6 all-reduce.2
where the time goes:
time: 1460 us; the launch traced here: 1450 us
  waiting for transfers between devices  846 us (58%)
  matrix products  177 us (12%)
  other arithmetic  163 us (11%)
  local copies, waits for them, and re-layouts  152 us (10%)
  blocking collectives  79.4 us (5%)
  loops' own time  16.4 us (1%)
  between operations  15.8 us (1%)
    unnamed x3, waiting for transfers between devices  649 us
    all_gather x1, waiting for transfers between devices, body(): codebook_all = lax.all_gather(codebook, 'dp', axis=0, tiled=True)  127 us
    add x18, other arithmetic, add_pair(): return first_term + second_term  99.5 us
    psum x1, blocking collectives, body(): histogram = lax.psum(local_counts, 'dp')  79.4 us
    ppermute x3, waiting for transfers between devices, shifted(): return lax.ppermute(block, axis, route)  70.1 us
    dot_general x8, matrix products, transposed_times(): lax.dot_general(first_term, second_term, (((0,), (0,)), ((), ())), prefer...  53.6 us
    unnamed x26, local copies, waits for them, and re-layouts  35.7 us
  transfers between devices with their start and end apart: 5, of which 3 were waited for; matrix products, arithmetic and copies ran while one was open for 8% of the time, Pallas kernels for 0%

commit v1 on v0

v1 whole, which is shorter than its diff:
```python
import functools
import math

import jax
import jax.numpy as jnp
from jax import lax
from jax.experimental import pallas as pl
from jax.experimental.pallas import tpu as pltpu
from jax.sharding import PartitionSpec as P

HEADS = 12
LANES = 128
TILE = 256
MESH = pl.DeviceIdType.MESH
MASKED = -1e30
GELU_SCALE = math.sqrt(2.0 / math.pi)
GELU_CUBIC = 0.044715


def times_transposed(first_term, second_term):
    return lax.dot_general(
        first_term, second_term, (((1,), (1,)), ((), ())), preferred_element_type=jnp.float32
    )


def transposed_times(first_term, second_term):
    return lax.dot_general(
        first_term, second_term, (((0,), (0,)), ((), ())), preferred_element_type=jnp.float32
    )


def times(first_term, second_term):
    return jnp.dot(first_term, second_term, preferred_element_type=jnp.float32)


def in_vmem():
    return pl.BlockSpec(memory_space=pltpu.VMEM)


def in_smem():
    return pl.BlockSpec(memory_space=pltpu.SMEM)


def in_place():
    return pl.BlockSpec(memory_space=pl.ANY)


def normalized(rows):
    row_mean = jnp.mean(rows, axis=-1, keepdims=True)
    centered = rows - row_mean
    variance = jnp.mean(centered * centered, axis=-1, keepdims=True)
    scale = lax.rsqrt(variance + 1e-06)
    return centered * scale, scale


def norm_backward(grad, hat, scale, gain_row):
    grad_hat = grad * gain_row
    first = jnp.mean(grad_hat, axis=-1, keepdims=True)
    second = jnp.mean(grad_hat * hat, axis=-1, keepdims=True)
    return scale * (grad_hat - first - hat * second)


def column_sum(rows):
    return jnp.sum(rows.astype(jnp.float32), axis=0, keepdims=True)


def fill_marks(lengths_ref, head_size, query_marks, key_marks):
    heads, rows, _ = query_marks.shape
    images = lengths_ref.shape[1]
    for head in range(heads):
        lane = lax.broadcasted_iota(jnp.int32, (1, LANES), 1) - (1 - head) * head_size
        inside = jnp.logical_and(lane >= 0, lane < images)
        for start in range(0, rows, LANES):
            positions = lax.broadcasted_iota(jnp.int32, (LANES, 1), 0) + start
            end, label = 0, jnp.zeros_like(positions)
            for image in range(images - 1):
                end = end + lengths_ref[lax.axis_index("section"), image]
                label = label + (positions >= end).astype(jnp.int32)
            same = label == lane
            other = jnp.logical_and(inside, jnp.logical_not(same))
            same = jnp.logical_and(inside, same)
            part = pl.ds(start, LANES)
            query_marks[head, part, :] = jnp.where(other, MASKED, 0.0).astype(jnp.bfloat16)
            key_marks[head, part, :] = jnp.where(same, 1.0, 0.0).astype(jnp.bfloat16)


def head_lanes(head, head_size, factor):
    lane = lax.broadcasted_iota(jnp.int32, (1, LANES), 1)
    inside = jnp.logical_and(lane >= head * head_size, lane < (head + 1) * head_size)
    return jnp.where(inside, factor, 0.0).astype(jnp.bfloat16)


def lane_block(index):
    return pl.ds(pl.multiple_of(index * LANES, LANES), LANES)


class Weights:
    def __init__(self, own_flag, own, other, held, sems):
        self.own_flag, self.own, self.other, self.held, self.sems = own_flag, own, other, held, sems

    def place(self, index):
        return self.held[index], self.sems.at[index]

    def start(self, index):
        @pl.when(self.own_flag == 1)
        def _():
            pltpu.make_async_copy(self.own[index], *self.place(index)).start()

        @pl.when(self.own_flag != 1)
        def _():
            pltpu.make_async_copy(self.other[index], *self.place(index)).start()

    def wait(self, index):
        pltpu.make_async_copy(self.own[index], *self.place(index)).wait()
        return self.place(index)[0]


def table_of(vectors, up_bias):
    width = vectors.shape[1]
    rows = jnp.concatenate([vectors, up_bias.reshape(-1, width)], axis=0).astype(jnp.float32)
    return jnp.pad(rows, ((0, -rows.shape[0] % 8), (0, 0)))


def up_bias_tile(table, first_row, j, width):
    per_row = width // TILE
    column = pl.multiple_of(j % per_row * TILE, TILE)
    return table[pl.ds(first_row + j // per_row, 1), pl.ds(column, TILE)]


VECTORS = 8
GROUP = 1 << 14
UNROLL = 4
SAVED = ("out", "hidden", "normed", "qkv", "mixed", "second", "slope", "act", "shown")


def saved_shapes(row_count, width, hidden_units):
    bfloat16, float32 = jnp.bfloat16, jnp.float32
    return [
        ((row_count, width), float32),
        ((row_count, width), float32),
        ((row_count, width), bfloat16),
        ((row_count, 3 * width), bfloat16),
        ((row_count, width), bfloat16),
        ((row_count, width), bfloat16),
        ((row_count, hidden_units), bfloat16),
        ((row_count, hidden_units), bfloat16),
        ((row_count, width), bfloat16),
    ]


def forward_steps(table, lengths_ref, rows_ref, stat_ref, buffers, work, weight, save, during):
    _, hidden_ref, normed_ref, qkv_ref, mixed_ref, second_ref = buffers[:6]
    query_marks, key_marks, max_columns, sum_columns = work
    rows, width = rows_ref.shape
    head_size = width // HEADS
    per_block = LANES // head_size
    half = rows // 2
    per_part = width // TILE

    fill_marks(lengths_ref, head_size, query_marks, key_marks)
    for start in range(0, rows, LANES):
        part = pl.ds(start, LANES)
        hat, _ = normalized(rows_ref[part, :].astype(jnp.float32))
        normed_ref[part, :] = (hat * (1.0 + table[0:1, :]) + table[1:2, :]).astype(jnp.bfloat16)
    save("normed")
    during("normed", 0)

    qkv_held = weight(0)
    for j in range(3 * per_part):
        columns = pl.ds(j * TILE, TILE)
        projected = times(normed_ref[...], qkv_held[:, columns])
        if j // per_part != 1:
            row = 2 + j // (2 * per_part)
            projected = projected + table[row : row + 1, pl.ds(j % per_part * TILE, TILE)]
        qkv_ref[:, columns] = projected.astype(jnp.bfloat16)

    save("qkv")
    during("qkv", 0)
    max_columns[...] = jnp.zeros_like(max_columns)
    sum_columns[...] = jnp.ones_like(sum_columns)

    @pl.loop(0, width // LANES)
    def _(i):
        keys = qkv_ref[:, lane_block(width // LANES + i)]
        values = qkv_ref[:, lane_block(2 * width // LANES + i)]
        lane = lax.broadcasted_iota(jnp.int32, (1, LANES), 1)
        keys_of = [keys * head_lanes(h, head_size, 1.0) + key_marks[h] for h in range(per_block)]
        values_of = [
            values * head_lanes(h, head_size, 1.0) + head_lanes(1 - h, head_size, 1.0) for h in range(per_block)
        ]
        units = [(start, h) for start in range(0, rows, half) for h in range(per_block)]

        def scores_of(unit):
            start, h = unit
            part = pl.ds(start, half)
            query = qkv_ref[part, lane_block(i)] * head_lanes(h, head_size, head_size**-0.5) + query_marks[h, part, :]
            return times_transposed(query, keys_of[h])

        ahead = scores_of(units[0])
        mixed = None
        for number, (start, h) in enumerate(units):
            part = pl.ds(start, half)
            scores = ahead
            if number + 1 < len(units):
                ahead = scores_of(units[number + 1])
            row_max = jnp.max(scores, axis=-1, keepdims=True)
            exponent = jnp.exp(scores - row_max).astype(jnp.bfloat16)
            sums = times(exponent, values_of[h])
            inside = jnp.logical_and(lane >= h * head_size, lane < (h + 1) * head_size)
            row_total = jnp.where(inside, pltpu.roll(sums, head_size, 1), sums)
            term = sums / row_total
            mixed = term if h == 0 else jnp.where(inside, term, mixed)
            here = lane == per_block * i + h
            max_columns[part, :] = jnp.where(here, row_max, max_columns[part, :])
            sum_columns[part, :] = jnp.where(here, row_total, sum_columns[part, :])
            if h == per_block - 1:
                mixed_ref[part, lane_block(i)] = mixed.astype(jnp.bfloat16)
        during("heads", i)

    save("mixed")
    stats = max_columns[...] + jnp.log(sum_columns[...])
    stat_ref[...] = jnp.transpose(stats)[: stat_ref.shape[0], :]

    out_held = weight(1)
    for start in range(0, width, TILE):
        columns = pl.ds(start, TILE)
        hidden_ref[:, columns] = (
            rows_ref[:, columns].astype(jnp.float32)
            + times(mixed_ref[...], out_held[:, columns])
            + table[4:5, columns]
        )
    save("hidden")
    for start in range(0, rows, LANES):
        part = pl.ds(start, LANES)
        hat, _ = normalized(hidden_ref[part, :])
        second_ref[part, :] = (hat * (1.0 + table[5:6, :]) + table[6:7, :]).astype(jnp.bfloat16)
    save("second")
    during("second", 0)


def up_product(table, second_ref, up_held, slope_ref, act_ref):
    tiles, width = up_held.shape[1] // TILE, second_ref.shape[1]

    @pl.loop(0, tiles // UNROLL)
    def _(group):
        def columns_of(j):
            return pl.ds(pl.multiple_of((group * UNROLL + j) * TILE, TILE), TILE)

        def pre_of(j):
            return times(second_ref[...], up_held[:, columns_of(j)])

        ahead = pre_of(0)
        for j in range(UNROLL):
            pre = ahead + up_bias_tile(table, VECTORS, group * UNROLL + j, width)
            if j + 1 < UNROLL:
                ahead = pre_of(j + 1)
            square = pre * pre
            bent = jnp.tanh(pre * (GELU_SCALE + (GELU_SCALE * GELU_CUBIC) * square))
            share = 0.5 + 0.5 * bent
            act_ref[:, columns_of(j)] = (pre * share).astype(jnp.bfloat16)
            steep = (0.5 - 0.5 * (bent * bent)) * (GELU_SCALE + (3.0 * GELU_SCALE * GELU_CUBIC) * square)
            slope_ref[:, columns_of(j)] = (share + pre * steep).astype(jnp.bfloat16)


def last_product(table, hidden_ref, act_ref, down_held, out_ref, shown_ref):
    for start in range(0, hidden_ref.shape[1], TILE):
        columns = pl.ds(start, TILE)
        result = hidden_ref[:, columns] + times(act_ref[...], down_held[:, columns]) + table[7:8, columns]
        if out_ref is not None:
            out_ref[:, columns] = result
        if shown_ref is not None:
            shown_ref[:, columns] = result.astype(jnp.bfloat16)


def forward_kernel(block, lengths_ref, rows_ref, tables_ref, *refs):
    own, other, made, (stat_ref,), held, buffers, work, (weight_sems, save_sems) = split_refs(
        refs, (4, 4, 9, 1, 4, 9, 4, 2)
    )
    weights = Weights((lax.axis_index("section") == block).astype(jnp.int32), own, other, held, weight_sems)
    for index in range(4):
        weights.start(index)
    saves = {
        name: pltpu.make_async_copy(source, target, save_sems.at[index])
        for index, (name, source, target) in enumerate(zip(SAVED, buffers, made))
    }
    table = tables_ref.at[block]
    forward_steps(
        table, lengths_ref, rows_ref, stat_ref, buffers, work, weights.wait,
        lambda name: saves[name].start(), lambda place, i: None,
    )
    up_product(table, buffers[5], weights.wait(2), buffers[6], buffers[7])
    last_product(table, buffers[1], buffers[7], weights.wait(3), buffers[0], buffers[8])
    for name in ("slope", "act", "out", "shown"):
        saves[name].start()
    for save in saves.values():
        save.wait()


def forward_work(row_count):
    return [
        pltpu.VMEM((2, row_count, LANES), jnp.bfloat16),
        pltpu.VMEM((2, row_count, LANES), jnp.bfloat16),
        pltpu.VMEM((row_count, LANES), jnp.float32),
        pltpu.VMEM((row_count, LANES), jnp.float32),
    ]


def forward_scratch(own, kept, row_count):
    return (
        [pltpu.VMEM(w.shape, w.dtype) for w in own]
        + [pltpu.VMEM(s, t) for s, t in kept]
        + forward_work(row_count)
        + [pltpu.SemaphoreType.DMA((4,)), pltpu.SemaphoreType.DMA((9,))]
    )


def forward_swap_kernel(lengths_ref, rows_ref, tables_ref, *refs):
    (
        own, other, (own_down,), made, (stat_ref, other_down), held, buffers, work,
        (own_held, other_held, weight_sems, save_sems, down_sems),
    ) = split_refs(refs, (3, 3, 1, 7, 2, 3, 8, 4, 5))
    section = lax.axis_index("section")
    barrier = pltpu.get_barrier_semaphore()
    pl.semaphore_signal(barrier, inc=1, device_id={"section": 1 - section}, device_id_type=MESH)
    weights = Weights((section == 1).astype(jnp.int32), own, other, held, weight_sems)
    for index in range(3):
        weights.start(index)
    down = pltpu.make_async_copy(own_down, own_held, down_sems.at[0])
    down.start()
    pl.semaphore_wait(barrier, 1)
    down.wait()
    swap = pltpu.make_async_remote_copy(
        src_ref=own_held, dst_ref=other_held, send_sem=down_sems.at[1], recv_sem=down_sems.at[2],
        device_id={"section": 1 - section}, device_id_type=MESH,
    )
    swap.start()
    saves = {
        name: pltpu.make_async_copy(source, target, save_sems.at[index])
        for index, (name, source, target) in enumerate(zip(SAVED[1:8], buffers[1:], made))
    }
    forward_steps(
        tables_ref.at[1], lengths_ref, rows_ref, stat_ref, buffers, work, weights.wait,
        lambda name: saves[name].start(), lambda place, i: None,
    )
    swap.wait()
    keep = pltpu.make_async_copy(other_held, other_down, down_sems.at[0])
    keep.start()
    up_product(tables_ref.at[1], buffers[5], weights.wait(2), buffers[6], buffers[7])
    saves["slope"].start()
    saves["act"].start()
    for save in saves.values():
        save.wait()
    keep.wait()


def forward_swap(lengths, rows, tables, own, other):
    row_count, width = rows.shape
    kept = saved_shapes(row_count, width, own[2].shape[1])[:8]
    shapes = kept[1:] + [((16, row_count), jnp.float32), (own[3].shape, own[3].dtype)]
    results = pl.pallas_call(
        forward_swap_kernel,
        out_shape=tuple(jax.ShapeDtypeStruct(s, t) for s, t in shapes),
        in_specs=[in_smem()] + [in_vmem()] * 2 + [in_place()] * 7,
        out_specs=[in_place()] * 7 + [in_vmem(), in_place()],
        scratch_shapes=[pltpu.VMEM(w.shape, w.dtype) for w in own[:3]]
        + [pltpu.VMEM(s, t) for s, t in kept]
        + forward_work(row_count)
        + [
            pltpu.VMEM(own[3].shape, own[3].dtype),
            pltpu.VMEM(own[3].shape, own[3].dtype),
            pltpu.SemaphoreType.DMA((4,)),
            pltpu.SemaphoreType.DMA((9,)),
            pltpu.SemaphoreType.DMA((3,)),
        ],
        compiler_params=pltpu.CompilerParams(
            collective_id=2, has_side_effects=True, vmem_limit_bytes=56 * 1024 * 1024
        ),
        name="forward_swap",
    )(lengths, rows, tables, *own[:3], *other, own[3])
    return results[:8], results[8]


def block_forward(block, lengths, rows, tables, own, other):
    row_count, width = rows.shape
    kept = saved_shapes(row_count, width, own[2].shape[1])
    stat_shape = (16, row_count)
    return pl.pallas_call(
        functools.partial(forward_kernel, block),
        out_shape=tuple(jax.ShapeDtypeStruct(s, t) for s, t in kept)
        + (jax.ShapeDtypeStruct(stat_shape, jnp.float32),),
        in_specs=[in_smem()] + [in_vmem()] * 2 + [in_place()] * 8,
        out_specs=[in_place()] * 9 + [in_vmem()],
        scratch_shapes=forward_scratch(own, kept, row_count),
        compiler_params=pltpu.CompilerParams(vmem_limit_bytes=56 * 1024 * 1024),
        cost_estimate=pl.CostEstimate(
            flops=2 * row_count * (12 * width * width + 2 * row_count * width),
            bytes_accessed=40 * 1024 * 1024,
            transcendentals=row_count * row_count * HEADS,
        ),
        name="block_forward",
    )(lengths, rows, tables, *own, *other)


def split_refs(refs, counts):
    groups, start = [], 0
    for count in counts:
        groups.append(refs[start : start + count])
        start = start + count
    return groups


def opening_kernel(real_shard, lengths_ref, code_tile_ref, vectors_ref, up_bias_ref, patches_ref, book_ref, *refs):
    (
        own, other, (tables_ref, all_codes_ref, chosen_ref), made, (stat_ref,), held, buffers, work,
        (weight_sems, save_sems),
        (rows_ref, book, total, half_out, half_in, table_in, code_slots, table_out, codes_ref),
        (load_sems, weight_send, weight_got, zero_send, zero_got, middle_send, middle_got, last_send, last_got,
         code_send, code_got, side_send, side_got, keep_sems),
    ) = split_refs(refs, (3, 3, 3, 7, 1, 3, 8, 4, 2, 9, 14))
    section, place = lax.axis_index("section"), lax.axis_index("dp")
    depth = book.shape[2]
    shard_rows, half_width = book.shape[3:]
    rows = rows_ref.shape[0]
    my_x, my_y, my_z = place % 2, place // 2 % 2, place // 4
    my_middle = my_y * (1 - section) + my_x * section
    my_last = my_x * (1 - section) + my_y * section
    middle_device = place + (1 - 2 * my_middle) * (2 - section)
    last_device = place + (1 - 2 * my_last) * (1 + section)

    barrier = pltpu.get_barrier_semaphore()
    pl.semaphore_signal(barrier, inc=1, device_id={"section": 1 - section}, device_id_type=MESH)
    for device in (middle_device, last_device):
        pl.semaphore_signal(barrier, inc=1, device_id={"dp": device}, device_id_type=MESH)
    for hop in range(1, depth):
        device = (my_z + hop) % depth * 4 + my_y * 2 + my_x
        pl.semaphore_signal(barrier, inc=1, device_id={"dp": device}, device_id_type=MESH)

    own_book = book.at[my_middle, my_last, my_z]
    load_book = pltpu.make_async_copy(
        book_ref.at[:, pl.ds(pl.multiple_of(section * half_width, LANES), half_width)], own_book, load_sems.at[0]
    )
    load_book.start()
    load_rows = pltpu.make_async_copy(
        patches_ref.at[pl.ds(pl.multiple_of(section * rows, rows), rows)], rows_ref, load_sems.at[1]
    )
    load_rows.start()
    own_codes = code_slots.at[my_z, my_middle, my_last]
    own_codes[...] = code_tile_ref[...]
    width = vectors_ref.shape[2]
    table_out[...] = jnp.zeros_like(table_out)
    table_out[:VECTORS, :] = vectors_ref[0].astype(jnp.float32)
    for j in range(up_bias_ref.shape[1] // width):
        table_out[VECTORS + j : VECTORS + j + 1, :] = up_bias_ref[:, j * width : (j + 1) * width].astype(jnp.float32)
    tables_ref[section] = table_out[...]
    codes = code_tile_ref[...]

    def shards_below(size):
        found = jnp.zeros_like(codes)
        for limit in range(size * real_shard, 4 * depth * real_shard, size * real_shard):
            found = found + (codes >= limit).astype(jnp.int32)
        return found

    holder, holder_z, holder_pair = shards_below(1), shards_below(4), shards_below(2)
    holder_y, holder_x = holder_pair - 2 * holder_z, holder - 2 * holder_pair
    holder_middle = holder_y * (1 - section) + holder_x * section
    holder_last = holder_x * (1 - section) + holder_y * section
    spot = (2 * holder_middle + holder_last) * GROUP + holder_z * shard_rows + codes - holder * real_shard
    turned = jnp.transpose(spot.astype(jnp.float32))
    for j in range(code_tile_ref.shape[0]):
        codes_ref[j * LANES : (j + 1) * LANES, :] = turned[:, j : j + 1].astype(jnp.int32)
    total[...] = jnp.zeros_like(total)

    def remote(source, land, send, got, **device):
        return pltpu.make_async_remote_copy(
            src_ref=source, dst_ref=land, send_sem=send, recv_sem=got, device_id=device, device_id_type=MESH
        )

    near = [sorted(range(depth), key=lambda z, here=here: (abs(z - here), z)) for here in range(depth)]

    def source_z(rank):
        found = my_z
        for here in range(depth):
            for other_rank in range(1, depth):
                here_now = jnp.logical_and(my_z == here, rank == other_rank)
                found = jnp.where(here_now, near[here][other_rank], found)
        return found

    def zero(source, target):
        part = book.at[my_middle, my_last, source]
        device = target * 4 + my_y * 2 + my_x
        return remote(part, part, zero_send.at[source, target], zero_got.at[source], dp=device)

    def zero_next(source):
        following = jnp.where(source < my_z, my_z + 1, my_z - 1)
        there = jnp.logical_and(following >= 0, following < depth)
        return jnp.clip(following, 0, depth - 1), there

    def zero_own(act):
        for step in (-1, 1):
            target = my_z + step
            there = jnp.logical_and(target >= 0, target < depth)

            @pl.when(there)
            def _():
                act(zero(my_z, jnp.clip(target, 0, depth - 1)))

    def middle(rank):
        source = source_z(rank)
        part = book.at[my_middle, my_last, source]
        return remote(part, part, middle_send.at[source], middle_got.at[source], dp=middle_device)

    def last(side, rank):
        source = source_z(rank)
        which = my_middle if side == 0 else 1 - my_middle
        part = book.at[which, my_last, source]
        return remote(part, part, last_send.at[side, source], last_got.at[side, source], dp=last_device)

    def codes_zero(hop):
        target = (my_z + hop) % depth * 4 + my_y * 2 + my_x
        return remote(own_codes, own_codes, code_send.at[hop - 1], code_got.at[hop - 1], dp=target)

    def codes_middle():
        part = code_slots.at[:, my_middle, my_last]
        return remote(part, part, code_send.at[depth], code_got.at[depth], dp=middle_device)

    def codes_last():
        part = code_slots.at[:, :, my_last]
        return remote(part, part, code_send.at[depth + 1], code_got.at[depth + 1], dp=last_device)

    def own_matrix(index):
        return pltpu.make_async_copy(own[index], held[index].at[section], weight_sems.at[index])

    def weight_across(index):
        part = held[index].at[section]
        return remote(part, part, weight_send.at[index], weight_got.at[index], section=1 - section)

    def keep(index):
        return pltpu.make_async_copy(held[index].at[1 - section], other[index], keep_sems.at[index])

    def send_matrix(index):
        own_matrix(index).wait()
        weight_across(index).start()

    table_across = remote(table_out, table_in, side_send.at[0], side_got.at[0], section=1 - section)
    half_across = remote(half_out, half_in, side_send.at[1], side_got.at[1], section=1 - section)

    def pick(which_middle, which_last):
        group = 2 * which_middle + which_last

        @pl.loop(0, total.shape[0] // rows)
        def _(block):
            part = pl.ds(pl.multiple_of(block * rows, rows), rows)
            inside = codes_ref[part, :] - group * GROUP
            lanes = lax.broadcasted_iota(jnp.int32, (1, depth * shard_rows), 1)
            hot = jnp.where(inside == lanes, 1.0, 0.0).astype(jnp.bfloat16)
            shards = book[which_middle, which_last].reshape(depth * shard_rows, half_width)
            total[part, :] = total[part, :] + times(hot, shards)

    for index in range(3):
        own_matrix(index).start()
    pl.semaphore_wait(barrier, 3 + depth - 1)
    table_across.start()
    load_book.wait()
    zero_own(lambda copy: copy.start())
    middle(0).start()
    last(0, 0).start()
    send_matrix(0)
    for hop in range(1, depth):
        codes_zero(hop).start()

    load_rows.wait()
    table_across.wait_recv()
    tables_ref[1 - section] = table_in[...]

    def weight(index):
        @pl.when(section == 1)
        def _():
            weight_across(index).wait_recv()
            keep(index).start()

        return held[index].at[0]

    def keep_late(index):
        @pl.when(section == 0)
        def _():
            weight_across(index).wait_recv()
            keep(index).start()

    saves = {
        name: pltpu.make_async_copy(source, target, save_sems.at[index])
        for index, (name, source, target) in enumerate(zip(SAVED[1:8], buffers[1:], made))
    }

    def from_zero(rank):
        source = source_z(rank)
        following, there = zero_next(source)
        zero(source, following).wait_recv()

        @pl.when(there)
        def _():
            zero(source, following).start()

        middle(rank).start()
        last(0, rank).start()

    def from_middle(rank):
        middle(rank).wait_recv()
        last(1, rank).start()

    def from_last(side):
        for rank in range(depth):
            last(side, rank).wait_recv()
        pick(my_middle if side == 0 else 1 - my_middle, 1 - my_last)

    def during(where, i):
        if where == "normed":
            from_zero(1)
            send_matrix(1)
            send_matrix(2)
        elif where == "qkv":
            from_middle(0)
            from_zero(2)
        elif where == "heads":

            @pl.when(i == 0)
            def _():
                from_middle(1)

            @pl.when(i == 1)
            def _():
                from_zero(3)

            @pl.when(i == 2)
            def _():
                from_middle(2)

            @pl.when(i == 3)
            def _():
                from_middle(3)

            @pl.when(i == 4)
            def _():
                pick(my_middle, my_last)

        elif where == "second":
            for hop in range(1, depth):
                codes_zero(hop).wait_recv()
            codes_middle().start()
            pick(1 - my_middle, my_last)

    forward_steps(
        tables_ref.at[0], lengths_ref, rows_ref, stat_ref, buffers, work, weight,
        lambda name: saves[name].start(), during,
    )
    table = tables_ref.at[0]
    keep_late(0)
    up_product(table, buffers[5], weight(2), buffers[6], buffers[7])
    saves["slope"].start()
    saves["act"].start()
    from_last(0)
    codes_middle().wait_recv()
    codes_last().start()
    keep_late(1)
    keep_late(2)
    from_last(1)
    own_rows = pl.ds(pl.multiple_of(section * rows, rows), rows)
    other_rows = pl.ds(pl.multiple_of((1 - section) * rows, rows), rows)
    half_out[...] = total[other_rows, :].astype(half_out.dtype)
    half_across.start()
    chosen_ref[:, pl.ds(pl.multiple_of(section * half_width, LANES), half_width)] = total[own_rows, :].astype(
        chosen_ref.dtype
    )
    half_across.wait_recv()
    chosen_ref[:, pl.ds(pl.multiple_of((1 - section) * half_width, LANES), half_width)] = half_in[...]
    codes_last().wait_recv()
    all_codes_ref[...] = code_slots[...]
    for index in range(3):
        weight_across(index).wait_send()
        keep(index).wait()
    table_across.wait_send()
    half_across.wait_send()
    zero_own(lambda copy: copy.wait_send())
    for hop in range(1, depth):
        source = source_z(hop)
        following, there = zero_next(source)

        @pl.when(there)
        def _():
            zero(source, following).wait_send()

        codes_zero(hop).wait_send()
    for hop in range(depth):
        middle(hop).wait_send()
        for side in range(2):
            last(side, hop).wait_send()
    codes_middle().wait_send()
    codes_last().wait_send()
    for save in saves.values():
        save.wait()


def opening(lengths, codes, vectors, up_bias, patches, codebook, own, devices, row_count):
    tokens, width = patches.shape
    half_width = width // 2
    depth, shard_rows = devices // 4, codebook.shape[0]
    padded = jnp.pad(codebook, ((0, -shard_rows % 16), (0, 0)))
    table_shape = (16, width)
    code_tile = codes.reshape(-1, LANES)
    kept = saved_shapes(row_count, width, own[2].shape[1])[:8]
    bfloat16, float32 = jnp.bfloat16, jnp.float32
    shapes = (
        [(w.shape, w.dtype) for w in own[:3]]
        + [
            ((2, *table_shape), float32),
            ((depth, 2, 2, *code_tile.shape), codes.dtype),
            ((row_count, width), bfloat16),
        ]
        + kept[1:]
        + [((16, row_count), float32)]
    )
    dma = pltpu.SemaphoreType.DMA
    results = pl.pallas_call(
        functools.partial(opening_kernel, shard_rows),
        out_shape=tuple(jax.ShapeDtypeStruct(s, t) for s, t in shapes),
        in_specs=[in_smem()] + [in_vmem()] * 3 + [in_place()] * 5,
        out_specs=[in_place()] * 3 + [in_vmem()] * 3 + [in_place()] * 7 + [in_vmem()],
        scratch_shapes=[pltpu.VMEM((2, *w.shape), w.dtype) for w in own[:3]] + forward_scratch((), kept, row_count)
        + [
            pltpu.VMEM((row_count, width), bfloat16),
            pltpu.VMEM((2, 2, depth, padded.shape[0], half_width), bfloat16),
            pltpu.VMEM((tokens, half_width), float32),
            pltpu.VMEM((row_count, half_width), bfloat16),
            pltpu.VMEM((row_count, half_width), bfloat16),
            pltpu.VMEM(table_shape, float32),
            pltpu.VMEM((depth, 2, 2, *code_tile.shape), codes.dtype),
            pltpu.VMEM(table_shape, float32),
            pltpu.VMEM((tokens, 1), jnp.int32),
            dma((2,)),
            dma((4,)),
            dma((4,)),
            dma((depth, depth)),
            dma((depth,)),
            dma((depth,)),
            dma((depth,)),
            dma((2, depth)),
            dma((2, depth)),
            dma((depth + 2,)),
            dma((depth + 2,)),
            dma((2,)),
            dma((2,)),
            dma((4,)),
        ],
        compiler_params=pltpu.CompilerParams(
            collective_id=1, has_side_effects=True, vmem_limit_bytes=60 * 1024 * 1024
        ),
        name="opening",
    )(lengths, code_tile, vectors, up_bias, patches, padded, *own[:3])
    return results[:3], results[3], results[4].reshape(devices, -1, LANES), results[5], results[6:]


def plain_opening(lengths, codes, table, patches, codebook, own, swapped, ordered, row_count):
    section = lax.axis_index("section")
    other = tuple(swapped(weight) for weight in own)
    tables = jnp.stack(ordered(table, swapped(table)))
    all_codes = lax.all_gather(codes, "dp", axis=0, tiled=True)
    half_width = patches.shape[1] // 2
    half_book = lax.dynamic_slice_in_dim(codebook, section * half_width, half_width, 1)
    half_book = lax.all_gather(half_book, "dp", axis=0, tiled=True)
    half_rows = jnp.take(half_book, codes, axis=0)

    def micro_rows(array, index):
        return lax.dynamic_slice_in_dim(array, index * row_count, row_count, 0)

    half_own = micro_rows(half_rows, section)
    half_other = swapped(micro_rows(half_rows, 1 - section))
    chosen = jnp.concatenate(ordered(half_own, half_other), axis=1)
    encoded = block_forward(0, lengths, micro_rows(patches, section), tables, own, other)
    return other, tables, all_codes, chosen, encoded


def backward_steps(from_code, lengths_ref, table, buffers, sums_ref, weight, arrived, save, during):
    (
        rows_ref, hidden_ref, qkv_ref, mixed_ref, slope_ref, stat_ref, branch_ref, attn_ref, projected_ref,
        grad_ref, second_ref, moved_ref, query_marks, key_marks,
    ) = buffers
    rows, width = rows_ref.shape
    hidden_units = slope_ref.shape[1]
    head_size = width // HEADS
    per_block = LANES // head_size
    half = rows // 2
    per_row = width // TILE
    sums_ref[...] = jnp.zeros_like(sums_ref)

    fill_marks(lengths_ref, head_size, query_marks, key_marks)
    arrived(("grads",))
    total = jnp.zeros((1, width), jnp.float32)
    for start in range(0, rows, LANES):
        part = pl.ds(start, LANES)
        grad = moved_ref[part, :].astype(jnp.float32)
        if from_code:
            grad = grad_ref[part, :] + 0.5 * (second_ref[part, :] - grad)
        grad_ref[part, :] = grad
        branch = grad.astype(jnp.bfloat16)
        branch_ref[part, :] = branch
        total = total + column_sum(branch)
    sums_ref[7:8, :] = total
    save("branch")
    during("branch")

    down_held = weight(3)
    arrived(("slope", "hidden"))

    def through_gelu(first, count):
        at_once = 3 if count % 3 == 0 else 1

        @pl.loop(0, count // at_once)
        def _(group):
            def tile_of(j):
                return first + group * at_once + j

            def block_of(j):
                return pl.ds(pl.multiple_of(tile_of(j) * TILE, TILE), TILE)

            def act_of(j):
                return times_transposed(branch_ref[...], down_held[block_of(j), :])

            ahead = act_of(0)
            for j in range(at_once):
                grad_act, block = ahead, block_of(j)
                if j + 1 < at_once:
                    ahead = act_of(j + 1)
                grad_pre = (grad_act * slope_ref[:, block].astype(jnp.float32)).astype(jnp.bfloat16)
                slope_ref[:, block] = grad_pre
                column = pl.multiple_of(tile_of(j) % per_row * TILE, TILE)
                sums_ref[pl.ds(VECTORS + tile_of(j) // per_row, 1), pl.ds(column, TILE)] = column_sum(grad_pre)

    tiles = hidden_units // TILE
    through_gelu(0, tiles // 4)
    during("gelu")
    through_gelu(tiles // 4, tiles - tiles // 4)
    save("pre")
    during("pre")
    up_held = weight(2)
    for start in range(0, width, TILE):
        block = pl.ds(start, TILE)
        second_ref[:, block] = times_transposed(slope_ref[...], up_held[block, :])
    during("second")

    gain_total, shift_total, attn_total = (jnp.zeros((1, width), jnp.float32) for _ in range(3))
    for start in range(0, rows, LANES):
        part = pl.ds(start, LANES)
        hat, scale = normalized(hidden_ref[part, :])
        grad = second_ref[part, :]
        gain_total = gain_total + column_sum(grad * hat)
        shift_total = shift_total + column_sum(grad)
        grad_hidden = grad_ref[part, :] + norm_backward(grad, hat, scale, 1.0 + table[5:6, :])
        grad_ref[part, :] = grad_hidden
        attn = grad_hidden.astype(jnp.bfloat16)
        attn_ref[part, :] = attn
        attn_total = attn_total + column_sum(attn)
    sums_ref[5:6, :] = gain_total
    sums_ref[6:7, :] = shift_total
    sums_ref[4:5, :] = attn_total
    save("attn")

    out_held = weight(1)
    for start in range(0, width, TILE):
        block = pl.ds(start, TILE)
        moved_ref[:, block] = times_transposed(attn_ref[...], out_held[block, :]).astype(jnp.bfloat16)
    during("attn")
    arrived(("mixed", "qkv", "stat"))

    def through_heads(first, count):
        @pl.loop(first, first + count)
        def _(i):
            query = qkv_ref[:, lane_block(i)]
            grad_mixed = moved_ref[:, lane_block(i)]
            products = jnp.transpose(
                grad_mixed.astype(jnp.float32) * mixed_ref[:, lane_block(i)].astype(jnp.float32)
            )
            mine = [head_lanes(h, head_size, 1.0) for h in range(per_block)]
            scaled = [head_lanes(h, head_size, head_size**-0.5) for h in range(per_block)]
            query_of = [query * scaled[h] for h in range(per_block)]
            marked_of = [query_of[h] + query_marks[h] for h in range(per_block)]
            grad_of = [grad_mixed * mine[h] for h in range(per_block)]
            row_dot = [
                jnp.sum(products[h * head_size : (h + 1) * head_size, :], axis=0, keepdims=True)
                for h in range(per_block)
            ]
            units = [(start, h) for start in range(0, rows, half) for h in range(per_block)]

            def products_of(unit):
                start, h = unit
                part = pl.ds(start, half)
                keys = qkv_ref[part, lane_block(width // LANES + i)]
                values = qkv_ref[part, lane_block(2 * width // LANES + i)]
                return (
                    times_transposed(keys * mine[h] + key_marks[h, part, :], marked_of[h]),
                    times_transposed(values, grad_of[h]),
                )

            ahead = products_of(units[0])
            grad_query = jnp.zeros((rows, LANES), jnp.float32)
            value_total = jnp.zeros((1, LANES), jnp.float32)
            for number, (start, h) in enumerate(units):
                part = pl.ds(start, half)
                scores, grad_probs = ahead
                if number + 1 < len(units):
                    ahead = products_of(units[number + 1])
                keys = qkv_ref[part, lane_block(width // LANES + i)]
                exact = jnp.exp(scores - stat_ref[pl.ds(per_block * i + h, 1), :])
                grad_scores = (exact * (grad_probs - row_dot[h])).astype(jnp.bfloat16)
                value_term = times(exact.astype(jnp.bfloat16), grad_of[h])
                key_term = times(grad_scores, query_of[h])
                grad_query = grad_query + transposed_times(grad_scores, keys * scaled[h])
                grad_value = value_term if h == 0 else grad_value + value_term
                grad_key = key_term if h == 0 else grad_key + key_term
                if h == per_block - 1:
                    grad_value = grad_value.astype(jnp.bfloat16)
                    projected_ref[part, lane_block(2 * width // LANES + i)] = grad_value
                    projected_ref[part, lane_block(width // LANES + i)] = grad_key.astype(jnp.bfloat16)
                    value_total = value_total + column_sum(grad_value)
            grad_query = grad_query.astype(jnp.bfloat16)
            projected_ref[:, lane_block(i)] = grad_query
            sums_ref[2:3, lane_block(i)] = column_sum(grad_query)
            sums_ref[3:4, lane_block(i)] = value_total

    groups = width // LANES
    for part in range(3):
        first, end = groups * part // 3, groups * (part + 1) // 3
        if end > first:
            through_heads(first, end - first)
        during(("heads", part))

    save("projected")
    qkv_held = weight(0)
    for start in range(0, width, TILE):
        grad_rows = None
        for j in range(3):
            term = times_transposed(
                projected_ref[:, j * width : (j + 1) * width], qkv_held[pl.ds(j * width + start, TILE), :]
            )
            grad_rows = term if grad_rows is None else grad_rows + term
        second_ref[:, pl.ds(start, TILE)] = grad_rows
    during("rows")

    arrived(("rows",))
    gain_total, shift_total = (jnp.zeros((1, width), jnp.float32) for _ in range(2))
    for start in range(0, rows, LANES):
        part = pl.ds(start, LANES)
        hat, scale = normalized(rows_ref[part, :].astype(jnp.float32))
        grad = second_ref[part, :]
        gain_total = gain_total + column_sum(grad * hat)
        shift_total = shift_total + column_sum(grad)
        grad_rows = grad_ref[part, :] + norm_backward(grad, hat, scale, 1.0 + table[0:1, :])
        grad_ref[part, :] = grad_rows if from_code else grad_rows.astype(jnp.bfloat16).astype(jnp.float32)
    sums_ref[0:1, :] = gain_total
    sums_ref[1:2, :] = shift_total
    save("grad")


class BackwardWeights(Weights):
    def place(self, index):
        return self.held[index - 1], self.sems.at[index - 1]

    def start(self, index):
        if index != 0:
            super().start(index)
            return
        width = self.own[0].shape[0]

        def begin(matrix):
            for j in range(3):
                block = pl.ds(j * width, width)
                pltpu.make_async_copy(
                    matrix[0].at[:, block], self.held[2].at[block, :], self.sems.at[3 + j]
                ).start()

        @pl.when(self.own_flag == 1)
        def _():
            begin(self.own)

        @pl.when(self.own_flag != 1)
        def _():
            begin(self.other)

    def wait(self, index):
        if index == 0:
            width = self.own[0].shape[0]
            for j in range(3):
                block = pl.ds(j * width, width)
                pltpu.make_async_copy(
                    self.own[0].at[:, block], self.held[2].at[block, :], self.sems.at[3 + j]
                ).wait()
            return self.held[2]
        return super().wait(index)


def backward_scratch(own, row_count):
    width, hidden_units = own[2].shape
    bfloat16, float32 = jnp.bfloat16, jnp.float32
    return [pltpu.VMEM(w.shape, w.dtype) for w in own[1:]] + [
        pltpu.VMEM((row_count, width), bfloat16),
        pltpu.VMEM((row_count, width), float32),
        pltpu.VMEM((row_count, 3 * width), bfloat16),
        pltpu.VMEM((row_count, width), bfloat16),
        pltpu.VMEM((row_count, hidden_units), bfloat16),
        pltpu.VMEM((16, row_count), float32),
        pltpu.VMEM((row_count, width), bfloat16),
        pltpu.VMEM((row_count, width), bfloat16),
        pltpu.VMEM((row_count, 3 * width), bfloat16),
        pltpu.VMEM((row_count, width), float32),
        pltpu.VMEM((row_count, width), float32),
        pltpu.VMEM((row_count, width), bfloat16),
        pltpu.VMEM((2, row_count, LANES), bfloat16),
        pltpu.VMEM((2, row_count, LANES), bfloat16),
        pltpu.SemaphoreType.DMA((6,)),
        pltpu.SemaphoreType.DMA((9,)),
    ]


def backward_loads(kept, grads_in, buffers, sems, whole_rows, whole_grad):
    rows_hbm, hidden_hbm, qkv_hbm, mixed_hbm, slope_hbm, stat_hbm = kept
    rows_ref, hidden_ref, qkv_ref, mixed_ref, slope_ref, stat_ref = buffers[:6]
    row_count = rows_ref.shape[0]
    mine = pl.ds(pl.multiple_of(lax.axis_index("section") * row_count, row_count), row_count)
    if whole_rows:
        rows_hbm = rows_hbm.at[mine, :]
    if len(grads_in) == 1 and not whole_grad:
        grad_pairs = [(grads_in[0], buffers[11])]
    elif whole_grad:
        grad_pairs = [(grads_in[0].at[mine, :], buffers[11])]
    else:
        grad_pairs = list(zip(grads_in, buffers[9:12]))
    pairs = {
        "slope": [(slope_hbm, slope_ref)], "hidden": [(hidden_hbm, hidden_ref)], "mixed": [(mixed_hbm, mixed_ref)],
        "qkv": [(qkv_hbm, qkv_ref)], "stat": [(stat_hbm, stat_ref)], "rows": [(rows_hbm, rows_ref)],
    }
    copies, index = {}, 0
    for name, entries in [("grads", grad_pairs), *pairs.items()]:
        copies[name] = []
        for source, target in entries:
            copies[name].append(pltpu.make_async_copy(source, target, sems.at[index]))
            index = index + 1
    return copies


def start_copies(copies):
    for copy in copies:
        copy.start()


def wait_copies(copies):
    for copy in copies:
        copy.wait()


def backward_kernel(block, lengths_ref, tables_ref, *refs):
    from_code = block == 0
    grads_in, kept, own, other, made, (sums_ref,), held, buffers, (weight_sems, load_sems, save_sems) = split_refs(
        refs, (3 if from_code else 1, 6, 4, 4, 5, 1, 3, 14, 3)
    )
    weights = BackwardWeights(
        (lax.axis_index("section") == block).astype(jnp.int32), own, other,
        held, weight_sems,
    )
    loads = backward_loads(kept, grads_in, buffers, load_sems, from_code, not from_code)
    saves = {
        name: pltpu.make_async_copy(source, target, save_sems.at[index])
        for index, (name, source, target) in enumerate(zip(
            ("grad", "branch", "pre", "attn", "projected"),
            (buffers[9], buffers[6], buffers[4], buffers[7], buffers[8]),
            made,
        ))
    }
    start_copies(loads["grads"])
    weights.start(3)
    start_copies(loads["slope"])
    weights.start(2)
    start_copies(loads["hidden"])
    weights.start(1)
    for name in ("mixed", "qkv", "stat", "rows"):
        start_copies(loads[name])

    def arrived(names):
        for name in names:
            wait_copies(loads[name])

    def during(where):
        if where == "pre":
            weights.start(0)

    backward_steps(
        from_code, lengths_ref, tables_ref.at[block], buffers, sums_ref, weights.wait, arrived,
        lambda name: saves[name].start(), during,
    )
    for save in saves.values():
        save.wait()


def block_backward(block, lengths, tables, grads_in, kept, own, other):
    row_count, width = kept[1].shape
    hidden_units = own[2].shape[1]
    bfloat16, float32 = jnp.bfloat16, jnp.float32
    made = [
        ((row_count, width), float32),
        ((row_count, width), bfloat16),
        ((row_count, hidden_units), bfloat16),
        ((row_count, width), bfloat16),
        ((row_count, 3 * width), bfloat16),
        (tables.shape[1:], float32),
    ]
    return pl.pallas_call(
        functools.partial(backward_kernel, block),
        out_shape=tuple(jax.ShapeDtypeStruct(s, t) for s, t in made),
        in_specs=[in_smem(), in_vmem()] + [in_place()] * (14 + len(grads_in)),
        out_specs=[in_place()] * 5 + [in_vmem()],
        scratch_shapes=backward_scratch(own, row_count) + [pltpu.SemaphoreType.DMA((5,))],
        compiler_params=pltpu.CompilerParams(vmem_limit_bytes=56 * 1024 * 1024),
        cost_estimate=pl.CostEstimate(
            flops=2 * row_count * (12 * width * width + 5 * row_count * width),
            bytes_accessed=40 * 1024 * 1024,
            transcendentals=row_count * row_count * HEADS,
        ),
        name="block_backward",
    )(lengths, tables, *grads_in, *kept, *own, *other)


SLOTS, HELD, RING, LAST_RING = 4, 6, 16, 12


def chunk_list(width, hidden_units):
    ups = hidden_units // width

    def of(block, operand, count):
        return [(block, operand, j) for j in range(count)]

    return (
        of(1, 3, ups) + of(1, 2, ups) + of(1, 1, 1) + of(1, 0, 3)
        + of(0, 3, ups) + of(0, 2, ups) + of(0, 1, 1) + of(0, 0, 3)
    )


def count_codes_in(codes_ref, code_count, counts_ref, stats_ref):
    high_count = counts_ref.shape[0]
    high_rows = -(-high_count // 16) * 16

    @pl.loop(0, codes_ref.shape[0], init_carry=jnp.zeros((high_rows, LANES), jnp.float32))
    def counts(block, total):
        codes = codes_ref[block]

        def hot(values, size):
            rows = lax.broadcasted_iota(jnp.int32, (size, 1), 0)
            pieces = [jnp.where(values[j : j + 1, :] == rows, 1.0, 0.0) for j in range(codes.shape[0])]
            return jnp.concatenate(pieces, axis=1).astype(jnp.bfloat16)

        return total + times_transposed(hot(codes >> 7, high_rows), hot(codes & (LANES - 1), LANES))

    counts = counts[:high_count, :]
    counts_ref[...] = counts.astype(jnp.int32)
    share = counts / float(codes_ref.shape[0] * codes_ref.shape[1] * LANES)
    used = counts > 0.0
    terms = jnp.where(used, share * jnp.log(jnp.where(used, share, 1.0)), 0.0)
    usage = jnp.sum(jnp.where(used, 1.0, 0.0), axis=(0, 1), keepdims=True) / code_count
    perplexity = jnp.exp(-jnp.sum(terms, axis=(0, 1), keepdims=True)) / code_count
    stats_ref[...] = jnp.concatenate([usage, perplexity], axis=1)


def closing_kernel(chunks, code_count, lengths_ref, tables_ref, codes_ref, *refs):
    (
        dec_grads_in, enc_grads_in, dec_kept, enc_kept, own, other, dec_left, enc_left,
        results, (vector_sums_ref, bias_sums_ref, counts_ref, stats_ref, shown_out, grads_out), held_weights, buffers,
        (weight_sems, load_sems, enc_weight_sems, enc_load_sems),
        (stage, zero, held, one, two, three, finals, fourth), (narrow, wide), (dec_grad_ref, dec_sums, enc_sums),
        (sums_send, sums_zero, sums_held, sums_first, sums_second, sums_third),
        (operand_sems, zero_send, zero_got, first_send, first_got, second_send, second_got, third_send, third_got,
         fourth_send, fourth_got, swap_sems, credit),
    ) = split_refs(refs, (1, 1, 6, 6, 4, 4, 3, 3, 4, 6, 3, 14, 4, 8, 2, 3, 6, 13))
    count = len(chunks)
    depth, share, width = stage.shape[1], stage.shape[4], stage.shape[5]
    half = width // 2
    rows = buffers[0].shape[0]
    ups = sum(1 for block, operand, _ in chunks if block == 0 and operand == 3)
    section, place = lax.axis_index("section"), lax.axis_index("dp")
    my_x, my_y, my_z = place % 2, place // 2 % 2, place // 4
    beside_x, beside_y = place + 1 - 2 * my_x, place + 2 - 4 * my_y
    first_device = beside_x * (1 - section) + beside_y * section
    second_device = beside_y * (1 - section) + beside_x * section
    own_half = pl.ds(pl.multiple_of(section * half, LANES), half)
    other_half = pl.ds(pl.multiple_of((1 - section) * half, LANES), half)

    barrier = pltpu.get_barrier_semaphore()
    pl.semaphore_signal(barrier, inc=1, device_id={"section": 1 - section}, device_id_type=MESH)
    for device in (beside_x, beside_y):
        pl.semaphore_signal(barrier, inc=1, device_id={"dp": device}, device_id_type=MESH)
    for hop in range(1, depth):
        device = (my_z + hop) % depth * 4 + my_y * 2 + my_x
        pl.semaphore_signal(barrier, inc=1, device_id={"dp": device}, device_id_type=MESH)

    operands = {
        0: (narrow.at[1], buffers[8]), 1: (buffers[3], buffers[7]), 2: (narrow.at[0], buffers[4]), 3: (wide, buffers[6]),
    }
    moves = {}
    for block, left in ((0, enc_left), (1, dec_left)):
        for operand, source in ((0, left[0]), (2, left[1]), (3, left[2])):
            moves[block, operand] = pltpu.make_async_copy(
                source, operands[operand][0], operand_sems.at[block, operand]
            )

    def matrices(block, sems):
        return BackwardWeights((section == block).astype(jnp.int32), own, other, held_weights, sems)

    dec_weights, enc_weights = matrices(1, weight_sems), matrices(0, enc_weight_sems)
    dec_loads = backward_loads(dec_kept, dec_grads_in, buffers, load_sems, False, True)
    enc_loads = backward_loads(enc_kept, enc_grads_in, buffers, enc_load_sems, True, False)
    start_copies(dec_loads["grads"])
    moves[1, 3].start()
    dec_weights.start(3)
    start_copies(dec_loads["slope"])
    dec_weights.start(2)
    moves[1, 2].start()
    start_copies(dec_loads["hidden"])
    dec_weights.start(1)
    for name in ("mixed", "qkv", "stat", "rows"):
        start_copies(dec_loads[name])
    moves[1, 0].start()
    pl.semaphore_wait(barrier, 3 + depth - 1)

    def remote(source, land, send, got, **device):
        return pltpu.make_async_remote_copy(
            src_ref=source, dst_ref=land, send_sem=send, recv_sem=got, device_id=device, device_id_type=MESH
        )

    def across(k):
        if k == count:
            return remote(sums_send, sums_zero, zero_send.at[k], zero_got.at[k], section=1 - section)
        return remote(
            stage.at[k % SLOTS, :, :, :, :, other_half], zero.at[k % SLOTS], zero_send.at[k], zero_got.at[k],
            section=1 - section,
        )

    def first(k):
        if k == count:
            return remote(sums_held, sums_first, first_send.at[k], first_got.at[k], dp=first_device)
        return remote(
            held.at[k % HELD, 1], one.at[k % RING], first_send.at[k], first_got.at[k], dp=first_device
        )

    def second(k):
        if k == count:
            return remote(sums_first, sums_second, second_send.at[k], second_got.at[k], dp=second_device)
        return remote(
            one.at[k % RING, 1], two.at[k % RING], second_send.at[k], second_got.at[k], dp=second_device
        )

    def third(k, hop):
        target = (my_z + hop) % depth
        device = target * 4 + my_y * 2 + my_x
        send, got = third_send.at[k, hop - 1], third_got.at[k, hop - 1]
        if k == count:
            return remote(sums_second, sums_third.at[hop - 1], send, got, dp=device)
        return remote(two.at[k % RING, target], three.at[k % LAST_RING, hop - 1], send, got, dp=device)

    def last(k):
        index = k % (count // 2)
        return remote(finals.at[index], fourth.at[index], fourth_send.at[k], fourth_got.at[k], section=1 - section)

    def send_across(k):
        if k >= SLOTS:
            pl.semaphore_wait(credit, 1)
        across(k).start()

    def give(k):
        if k == count:
            dec, enc = dec_sums[...], enc_sums[...]
            sums_held[...] = jnp.where(section == 0, enc, dec)
            sums_send[...] = jnp.where(section == 0, dec, enc)
            across(k).start()
            return
        block, operand, j = chunks[k]
        key = (block, operand)
        if operand == 3 and j != 0:
            send_across(k)
            return
        if j == 0 and key in moves and key != (0, 3):
            moves[key].wait()
        made = range(k, k + ups) if operand == 3 else range(k, k + 1)
        for each in made:
            if each >= SLOTS:
                across(each - SLOTS).wait_send()
        left, right = operands[operand]
        if operand == 3:

            @pl.loop(0, depth)
            def _(tile):
                columns = pl.ds(pl.multiple_of(tile * 4 * ups * share, LANES), 4 * ups * share)
                product = transposed_times(left[:, columns], right[...]).astype(stage.dtype)
                product = product.reshape(2, 2, ups, share, width)
                for j in range(ups):
                    stage[(k + j) % SLOTS, tile] = product[:, :, j]

        else:
            product = transposed_times(left[...], right[:, j * width : (j + 1) * width]).astype(stage.dtype)
            stage[k % SLOTS] = product.reshape(depth, 2, 2, share, width)
        send_across(k)
        last_of_key = operand == 3 or k + 1 == count or chunks[k + 1][:2] != key
        if last_of_key and block == 1 and operand in (0, 2):
            moves[0, operand].start()

    def begin(k):
        across(k).wait_recv()
        if k == count:
            sums_held[...] = sums_held[...] + sums_zero[...]
            first(k).start()
            return
        if k >= HELD:
            first(k - HELD).wait_send()
        slot = k % SLOTS
        for a in range(2):
            for b in range(2):
                chip_x = (my_x + (a * (1 - section) + b * section)) % 2
                chip_y = (my_y + (b * (1 - section) + a * section)) % 2
                held[k % HELD, a, b] = stage[slot, :, chip_y, chip_x, :, own_half] + zero[slot, :, chip_y, chip_x]
        first(k).start()
        if k + SLOTS < count:
            pl.semaphore_signal(credit, inc=1, device_id={"section": 1 - section}, device_id_type=MESH)

    def after_first(k):
        first(k).wait_recv()
        if k == count:
            first(k).wait_send()
            sums_first[...] = sums_first[...] + sums_held[...]
        else:
            slot = k % RING
            one[slot] = one[slot] + held[k % HELD, 0]
        second(k).start()

    def after_second(k):
        second(k).wait()
        if k == count:
            sums_second[...] = sums_second[...] + sums_first[...]
        else:
            slot = k % RING
            two[slot] = two[slot] + one[slot, 0]
        for hop in range(1, depth):
            third(k, hop).start()

    def after_third(k):
        if k == count:
            total = sums_second[...]
            for hop in range(1, depth):
                third(k, hop).wait()
                total = total + sums_third[hop - 1]
            vector_sums_ref[...] = total[:VECTORS, :]
            bias_sums_ref[...] = jnp.zeros_like(bias_sums_ref)
            for j in range(ups):
                bias_sums_ref[0:1, j * width : (j + 1) * width] = total[VECTORS + j : VECTORS + j + 1, :]
            return
        block = chunks[k][0]
        slot = k % RING
        total = two[slot, my_z].astype(jnp.float32)
        for hop in range(1, depth):
            third(k, hop).wait()
            total = total + three[k % LAST_RING, hop - 1].astype(jnp.float32)

        @pl.when(section == block)
        def _():
            put(k, total, own_half, section * half)

        @pl.when(section != block)
        def _():
            finals[k % (count // 2)] = total
            last(k).start()

    def put(k, total, lanes, offset):
        _, operand, j = chunks[k]
        if operand == 3:
            results[3][j * share : (j + 1) * share, lanes] = total
        else:
            start = pl.multiple_of(j * width + offset, LANES)
            results[operand][:, pl.ds(start, half)] = total

    def after_fourth(k):
        if k == count:
            return
        block = chunks[k][0]

        @pl.when(section == block)
        def _():
            last(k).wait_recv()
            put(k, fourth[k % (count // 2)], other_half, (1 - section) * half)

        @pl.when(section != block)
        def _():
            last(k).wait_send()

    phases = ((1, begin), (0, give), (3, after_first), (5, after_second), (7, after_third), (8, after_fourth))

    def step(number):
        for phase, action in phases:
            for k in range(count + 1):
                if min(k, count - 1) // 2 + phase == number:
                    action(k)

    mine = pl.ds(pl.multiple_of(section * rows, rows), rows)

    def deliver(block, source, target, sem, start):
        stay = pltpu.make_async_copy(source, target.at[mine, :], swap_sems.at[sem, 0])
        go = remote(source, target.at[mine, :], swap_sems.at[sem, 1], swap_sems.at[sem, 2], section=1 - section)

        @pl.when(section == block)
        def _():
            if start:
                stay.start()
            else:
                stay.wait()
                go.wait_recv()

        @pl.when(section != block)
        def _():
            if start:
                go.start()
            else:
                go.wait_send()

    branch_buffer, grad_buffer, second_buffer = buffers[6], buffers[9], buffers[10]
    shown_dec = (1, branch_buffer, shown_out, 0)
    grads_dec = (1, dec_grad_ref, grads_out, 1)
    shown_enc = (0, branch_buffer, shown_out, 2)
    grads_enc = (0, grad_buffer, grads_out, 3)

    def once(act):
        seen = set()

        def acted(name):
            if name not in seen:
                seen.add(name)
                act(name)

        return acted

    dec_arrive = once(lambda name: wait_copies(dec_loads[name]))
    enc_arrive = once(lambda name: wait_copies(enc_loads[name]))
    enc_matrix = once(lambda index: enc_weights.wait(index))

    def enc_weight(index):
        enc_matrix(index)
        return held_weights[2] if index == 0 else enc_weights.place(index)[0]

    def dec_arrived(names):
        for name in names:
            dec_arrive(name)

    def enc_arrived(names):
        for name in names:
            enc_arrive(name)
        if "grads" in names:
            enc_arrive("hidden")
            moves[0, 3].wait()
            last_product(tables_ref.at[0], buffers[1], wide, enc_weight(3), second_buffer, None)

    dec_steps = {"branch": 0, "gelu": 1, "pre": 2, "attn": 3, ("heads", 2): 4, "rows": 5}
    enc_steps = {"branch": 6, "gelu": 7, "pre": 8, ("heads", 0): 9, ("heads", 2): 10}

    def during_decoder(where):
        if where == "pre":
            last_product(tables_ref.at[1], buffers[1], wide, held_weights[2], None, branch_buffer)
            deliver(*shown_dec, True)
            dec_weights.start(0)
            moves[0, 3].start()
        if where in dec_steps:
            step(dec_steps[where])
        if where == "second":
            enc_weights.start(2)
        elif where == "attn":
            start_copies(enc_loads["slope"])
            start_copies(enc_loads["hidden"])
            enc_weights.start(1)
        elif where == ("heads", 2):
            for name in ("mixed", "qkv", "stat"):
                start_copies(enc_loads[name])
        elif where == "rows":
            enc_weights.start(3)

    def during_encoder(where):
        if where == "pre":
            branch_buffer[...] = second_buffer[...].astype(branch_buffer.dtype)
            deliver(*shown_enc, True)
            enc_weights.start(0)
        if where in enc_steps:
            step(enc_steps[where])

    def nothing(name):
        return None

    backward_steps(
        False, lengths_ref, tables_ref.at[1], buffers, dec_sums, dec_weights.wait, dec_arrived, nothing,
        during_decoder,
    )
    start_copies(enc_loads["grads"])
    start_copies(enc_loads["rows"])
    dec_grad_ref[...] = grad_buffer[...]
    deliver(*grads_dec, True)
    deliver(*shown_dec, False)
    backward_steps(
        True, lengths_ref, tables_ref.at[0], buffers, enc_sums, enc_weight, enc_arrived, nothing, during_encoder,
    )
    deliver(*grads_enc, True)
    for number in range(11, (count - 1) // 2 + 9):
        step(number)
        if number == 13:
            count_codes_in(codes_ref, code_count, counts_ref, stats_ref)
    for parts in (grads_dec, shown_enc, grads_enc):
        deliver(*parts, False)
    for k in range(count + 1):
        if k + SLOTS >= count:
            across(k).wait_send()
        if k != count and k + HELD >= count:
            first(k).wait_send()


def closing(lengths, tables, codes, code_count, cotangent, enc_grads_in, dec_kept, enc_kept, own, other, dec_left, enc_left, devices):
    row_count, width = dec_kept[0].shape
    hidden_units = own[2].shape[1]
    chunks = chunk_list(width, hidden_units)
    count, depth, share, half = len(chunks), devices // 4, width // devices, width // 2
    bfloat16, float32 = jnp.bfloat16, jnp.float32
    tokens = cotangent.shape[0]
    table = pltpu.VMEM(tables.shape[1:], float32)
    dma = pltpu.SemaphoreType.DMA
    shapes = [
        ((share, 3 * width), float32),
        ((share, width), float32),
        ((share, hidden_units), float32),
        ((hidden_units // devices, width), float32),
        ((VECTORS, width), float32),
        ((8, hidden_units), float32),
        ((-(-code_count // LANES), LANES), jnp.int32),
        ((1, 2), float32),
        ((tokens, width), bfloat16),
        ((tokens, width), float32),
    ]
    return pl.pallas_call(
        functools.partial(closing_kernel, chunks, code_count),
        out_shape=tuple(jax.ShapeDtypeStruct(s, t) for s, t in shapes),
        in_specs=[in_smem()] + [in_vmem()] * 2 + [in_place()] * 28,
        out_specs=[in_vmem()] * 8 + [in_place()] * 2,
        scratch_shapes=backward_scratch(own, row_count)
        + [
            dma((6,)),
            dma((9,)),
            pltpu.VMEM((SLOTS, depth, 2, 2, share, width), bfloat16),
            pltpu.VMEM((SLOTS, depth, 2, 2, share, half), bfloat16),
            pltpu.VMEM((HELD, 2, 2, depth, share, half), bfloat16),
            pltpu.VMEM((RING, 2, depth, share, half), bfloat16),
            pltpu.VMEM((RING, depth, share, half), bfloat16),
            pltpu.VMEM((LAST_RING, depth - 1, share, half), bfloat16),
            pltpu.VMEM((count // 2, share, half), float32),
            pltpu.VMEM((count // 2, share, half), float32),
            pltpu.VMEM((2, row_count, width), bfloat16),
            pltpu.VMEM((row_count, hidden_units), bfloat16),
            pltpu.VMEM((row_count, width), float32),
            table,
            table,
            table,
            table,
            table,
            table,
            table,
            pltpu.VMEM((depth - 1, *tables.shape[1:]), float32),
            dma((2, 4)),
        ]
        + [dma((count + 1,))] * 6
        + [dma((count + 1, depth - 1))] * 2
        + [dma((count,))] * 2
        + [dma((4, 3)), pltpu.SemaphoreType.REGULAR],
        compiler_params=pltpu.CompilerParams(
            collective_id=0, has_side_effects=True, vmem_limit_bytes=62 * 1024 * 1024
        ),
        name="closing",
    )(lengths, tables, codes, cotangent, *enc_grads_in, *dec_kept, *enc_kept, *own, *other, *dec_left, *enc_left)


def finish_kernel(vectors_ref, bias_ref, *refs):
    sources, targets, (bias_out, vectors_out), held, (in_sems, out_sems) = split_refs(refs, (6, 6, 2, 6, 2))
    loads = [pltpu.make_async_copy(s, h, in_sems.at[i]) for i, (s, h) in enumerate(zip(sources, held))]
    saves = [pltpu.make_async_copy(h, t, out_sems.at[i]) for i, (h, t) in enumerate(zip(held, targets))]
    start_copies(loads)
    place = lax.axis_index("dp")

    def from_place(ref, out):
        whole, part = ref.shape[1], out.shape[1]
        turned = pltpu.roll(ref[...], (whole - place * part) % whole, 1)
        out[...] = turned[: out.shape[0], :part]

    from_place(vectors_ref, vectors_out)
    from_place(bias_ref, bias_out)
    for load, save in zip(loads, saves):
        load.wait()
        save.start()
    wait_copies(saves)


def finish(results, vector_sums, bias_sums, devices):
    small = [
        jax.ShapeDtypeStruct((1, bias_sums.shape[1] // devices), jnp.float32),
        jax.ShapeDtypeStruct((VECTORS, vector_sums.shape[1] // devices), jnp.float32),
    ]
    return pl.pallas_call(
        finish_kernel,
        out_shape=tuple(jax.ShapeDtypeStruct(a.shape, a.dtype) for a in results) + tuple(small),
        in_specs=[in_vmem()] * 2 + [in_place()] * 6,
        out_specs=[in_place()] * 6 + [in_vmem()] * 2,
        scratch_shapes=[pltpu.VMEM(a.shape, a.dtype) for a in results]
        + [pltpu.SemaphoreType.DMA((6,)), pltpu.SemaphoreType.DMA((6,))],
        compiler_params=pltpu.CompilerParams(vmem_limit_bytes=60 * 1024 * 1024),
        name="finish",
    )(vector_sums, bias_sums, *results)


def count_codes(all_codes, code_count):
    high = -(-code_count // LANES)
    high_hot = (all_codes[:, None] // LANES == jnp.arange(high, dtype=jnp.int32)).astype(jnp.bfloat16)
    low_hot = (all_codes[:, None] % LANES == jnp.arange(LANES, dtype=jnp.int32)).astype(jnp.bfloat16)
    counts = transposed_times(high_hot, low_hot)
    return counts.reshape(-1)[:code_count].astype(jnp.int32)


def code_statistics(histogram, rows):
    code_share = histogram.astype(jnp.float32) / rows
    is_used = histogram > 0
    usage_share = jnp.mean(is_used.astype(jnp.float32))
    entropy = -jnp.sum(
        jnp.where(is_used, code_share * jnp.log(jnp.where(is_used, code_share, 1.0)), 0.0)
    )
    return jnp.stack([usage_share, jnp.exp(entropy) / histogram.shape[0]])


def plain_closing(
    is_first, lengths, tables, cotangent, enc_grads_in, dec_kept, enc_kept, own, other, encoded, decoded, shown,
    swapped, ordered, vector_count, width,
):
    code_grad, dec_branch, dec_pre, dec_attn, dec_projected, dec_sums = block_backward(
        1, lengths, tables, (cotangent,), dec_kept, own, other
    )
    grad, branch, pre, attn, projected, enc_sums = block_backward(
        0, lengths, tables, (code_grad, *enc_grads_in), enc_kept, own, other
    )
    encoder = ((encoded[1], encoded[3], encoded[4], encoded[6]), (projected, attn, pre, branch))
    decoder = ((decoded[1], decoded[3], decoded[4], decoded[6]), (dec_projected, dec_attn, dec_pre, dec_branch))
    results = []
    for index in range(4):
        enc = transposed_times(encoder[0][index], encoder[1][index])
        dec = transposed_times(decoder[0][index], decoder[1][index])
        results.append(jnp.where(is_first, enc, dec) + swapped(jnp.where(is_first, dec, enc)))
    own_sums, other_sums = ordered(enc_sums, dec_sums)
    sums = own_sums + swapped(other_sums)
    bias_rows = own[2].shape[1] // width
    results = results + [sums[vector_count : vector_count + bias_rows].reshape(-1), sums[:vector_count]]
    weight_grads = tuple(
        lax.psum_scatter(part, "dp", scatter_dimension=axis, tiled=True)
        for part, axis in zip(results, (0, 0, 0, 0, 0, 1))
    )

    def both_micro(enc_rows, dec_rows):
        own_rows, other_rows = ordered(enc_rows, dec_rows)
        return jnp.concatenate(ordered(own_rows, swapped(other_rows)), axis=0)

    return weight_grads, both_micro(*shown), both_micro(grad, code_grad)


def body(
    patches,
    cotangent,
    codes,
    lengths,
    codebook,
    qkv_weight,
    out_weight,
    up_weight,
    down_weight,
    up_bias,
    vectors,
):
    section_index = lax.axis_index("section")
    is_first = section_index == 0
    devices = lax.axis_size("dp")
    tok_rows, model_width = patches.shape
    row_count = tok_rows // lengths.shape[0]
    code_count = codebook.shape[0] * devices

    def swapped(array):
        return lax.ppermute(array, "section", [(0, 1), (1, 0)])

    def ordered(own, other):
        return jnp.where(is_first, own, other), jnp.where(is_first, other, own)

    own = (qkv_weight[0], out_weight[0], up_weight[0], down_weight[0])
    if devices == 16:
        other, tables, all_codes, chosen, encoded = opening(
            lengths, codes, vectors, up_bias, patches, codebook, own, devices, row_count
        )
        decoded, other_down = forward_swap(lengths, chosen, tables, own, other)
        other = (*other, other_down)
    else:
        other, tables, all_codes, chosen, encoded = plain_opening(
            lengths, codes, table_of(vectors[0], up_bias[0]), patches, codebook, own, swapped, ordered, row_count
        )
        decoded = block_forward(1, lengths, chosen, tables, own, other)
        shown = (encoded[8], decoded[8])
        enc_grads_in = (encoded[0], chosen)
        encoded, decoded = ((*made[1:8], made[9]) for made in (encoded, decoded))

    def saved(rows, made):
        hidden, _, projected, mixed, _, slope, _, stats = made
        return rows, hidden, projected, mixed, slope, stats

    if devices == 16:
        *weight_grads, vector_sums, bias_sums, counts, code_stats, outputs, input_grad = closing(
            lengths, tables, all_codes, code_count, cotangent, (chosen,), saved(chosen, decoded),
            saved(patches, encoded), own, other, (decoded[1], decoded[4], decoded[6]),
            (encoded[1], encoded[4], encoded[6]), devices,
        )
        histogram, code_stats = counts.reshape(-1)[:code_count], code_stats[0]
        *weight_grads, outputs, input_grad, bias_grad, vector_grad = finish(
            (*weight_grads, outputs, input_grad), vector_sums, bias_sums, devices
        )
        weight_grads = (*weight_grads, bias_grad[0], vector_grad)
    else:
        histogram = count_codes(all_codes, code_count)
        code_stats = code_statistics(histogram, tok_rows * devices)
        weight_grads, outputs, input_grad = plain_closing(
            is_first, lengths, tables, cotangent, enc_grads_in, saved(chosen, decoded), saved(patches, encoded), own,
            other, encoded, decoded, shown, swapped, ordered, vectors.shape[1], model_width,
        )
    return (outputs[None], input_grad[None], *(part[None] for part in weight_grads), histogram, code_stats)


def solution(mesh):
    placed = (
        P("dp", None),
        P("dp", None),
        P("dp"),
        P("dp", None),
        P("dp", None),
        P("section", None, None),
        P("section", None, None),
        P("section", None, None),
        P("section", None, None),
        P("section", None),
        P("section", None, None),
    )
    return jax.shard_map(
        body,
        mesh=mesh,
        in_specs=placed,
        out_specs=(
            P("section", "dp", None),
            P("section", "dp", None),
            P("section", "dp", None),
            P("section", "dp", None),
            P("section", "dp", None),
            P("section", "dp", None),
            P("section", "dp"),
            P("section", None, "dp"),
            P(),
            P(),
        ),
        check_vma=False,
    )
```

time: 1460 us -> 262 us (0.18)
  waiting for transfers between devices: 846 us -> 0 us
  Pallas kernels: 0 us -> 254 us
  matrix products: 177 us -> 0 us
  other arithmetic: 163 us -> 0 us
  local copies, waits for them, and re-layouts: 152 us -> 3.07 us
  blocking collectives: 79.4 us -> 0 us
  loops' own time: 16.4 us -> 0 us
  between operations: 15.8 us -> 1.14 us
    unnamed x3 -> x0, waiting for transfers between devices: 649 us -> none
    pallas_call x0 -> x4, Pallas kernels: none -> 254 us  [the longest x1 158 us: closing(): pl.pallas_call(functools.partial(closing_kernel, chunks, code_count), out...]
    dot_general x36 -> x0, matrix products: 177 us -> none  [the longest x8 53.6 us: transposed_times(): lax.dot_general(first_term, second_term, (((0,), (0,)), ((), ())), prefer...]
    all_gather x1 -> x0, waiting for transfers between devices: 127 us -> none  [body(): codebook_all = lax.all_gather(codebook, 'dp', axis=0, tiled=True)]
    add x22 -> x0, other arithmetic: 102 us -> none  [the longest x18 99.5 us: add_pair(): return first_term + second_term]
    psum x1 -> x0, blocking collectives: 79.4 us -> none  [body(): histogram = lax.psum(local_counts, 'dp')]
    ppermute x3 -> x0, waiting for transfers between devices: 70.1 us -> none  [shifted(): return lax.ppermute(block, axis, route)]
    unnamed x26 -> x6, local copies, waits for them, and re-layouts: 35.7 us -> 1.13 us
  transfers between devices with their start and end apart: 5 -> 0, of which waited for: 3 -> 0; matrix products, arithmetic and copies ran while one was open for 8% -> 0% of each run, Pallas kernels for 0% -> 0%
where the time goes in v1:
time: 262 us; the launch traced here: 259 us
  Pallas kernels  254 us (97%)
  local copies, waits for them, and re-layouts  3.07 us (1%)
    pallas_call x1, Pallas kernels, closing(): pl.pallas_call(functools.partial(closing_kernel, chunks, code_count), out...  158 us
    pallas_call x1, Pallas kernels, opening(): pl.pallas_call(functools.partial(opening_kernel, shard_rows), out_shape=t...  62.3 us
    pallas_call x1, Pallas kernels, forward_swap(): pl.pallas_call(forward_swap_kernel, out_shape=tuple((jax.ShapeDtypeStruct...  27 us
    pallas_call x1, Pallas kernels, finish(): pl.pallas_call(finish_kernel, out_shape=tuple((jax.ShapeDtypeStruct(a.sha...  7.44 us

profile of v1, /device:TPU:0, one launch (start us, length us, event | category | flops | bytes accessed | tf_op | source)
XLA Modules:
  0.0 258.7 jit_solution(1173667662420284302)
XLA Ops:
  0.6 1.9 pad.4.book_ref
  2.6 62.3 %opening.1 = (bf16[768,2304]{1,0:T(8,128)(2,1)}, bf16[768,768]{1,0:T(8,128)(2,1)}, bf16[768,3072]{1,0:T(8,128)(2,1)}, f32[2,16,768]{2,1,0:T(8,128)}, s32[4,2,2,8...) custom-call(s32[2,4]{1,0:T(2,128)} %lengths_ref.5, ...), custom_call_target="tpu_custom_call" | custom-call | tf_op jit(solution)/shard_map/opening/pallas_call | solution.py:722
  64.9 27.0 %forward_swap.1 = (f32[512,768]{1,0:T(8,128)}, bf16[512,768]{1,0:T(8,128)(2,1)}, bf16[512,2304]{1,0:T(8,128)(2,1)}, bf16[512,768]{1,0:T(8,128)(2,1)}, bf16[512,7...) custom-call(s32[2,4]{1,0:T(2,128)} %lengths_ref.5, ...), custom_call_target="tpu_custom_call" | custom-call | tf_op jit(solution)/shard_map/forward_swap/pallas_call | solution.py:360
  91.9 157.7 %closing.1 = (f32[48,2304]{1,0:T(8,128)}, f32[48,768]{1,0:T(8,128)}, f32[48,3072]{1,0:T(8,128)}, f32[192,768]{1,0:T(8,128)}, f32[8,768]{1,0:T(8,128)}, /*index=5...) custom-call(s32[2,4]{1,0:T(2,128)} %lengths_ref.5, ...), custom_call_target="tpu_custom_call" | custom-call | tf_op jit(solution)/shard_map/closing/pallas_call | solution.py:1543
  249.6 0.0 copy-start
  249.6 0.0 copy-start.1
  249.6 7.4 %finish.1 = (f32[48,2304]{1,0:T(8,128)}, f32[48,768]{1,0:T(8,128)}, f32[48,3072]{1,0:T(8,128)}, f32[192,768]{1,0:T(8,128)}, bf16[1024,768]{1,0:T(8,128)(2,1)}, /...) custom-call(f32[8,768]{1,0:T(8,128)} %get-tuple-element.74.vectors_ref, ...), custom_call_target="tpu_custom_call" | custom-call | tf_op jit(solution)/shard_map/finish/pallas_call | solution.py:1609
  257.1 0.0 copy-done
  257.1 0.6 copy.23
  257.7 0.0 copy-done.1
  257.7 0.5 copy.24
Async XLA Ops:
  249.6 7.5 %copy-start = (s32[50,128]{1,0:T(8,128)S(1)}, s32[50,128]{1,0:T(8,128)}, u32[]{:S(2)}) copy-start(s32[50,128]{1,0:T(8,128)} %get-tuple-element.90) | copy-start | bytes 76804
  249.6 8.1 %copy-start.1 = (f32[1,2]{1,0:T(1,128)S(1)}, f32[1,2]{1,0:T(1,128)}, u32[]{:S(2)}) copy-start(f32[1,2]{1,0:T(1,128)} %get-tuple-element.91) | copy-start | bytes 28

commit v2 on v1

--- a/solution.py
+++ b/solution.py
@@ -130,6 +130,7 @@
 VECTORS = 8
 GROUP = 1 << 14
 UNROLL = 4
+PIECES = 3
 SAVED = ("out", "hidden", "normed", "qkv", "mixed", "second", "slope", "act", "shown")
 
 
@@ -148,9 +149,18 @@
     ]
 
 
+def turned_sources(buffers, work):
+    out, hidden, _, qkv, mixed, _, *rest = buffers
+    return (out, hidden, work[4], qkv, mixed, work[5], *rest)
+
+
+def turned_shapes(kept):
+    return [((shape[1], shape[0]), kind) if index in (2, 5) else (shape, kind) for index, (shape, kind) in enumerate(kept)]
+
+
 def forward_steps(table, lengths_ref, rows_ref, stat_ref, buffers, work, weight, save, during):
     _, hidden_ref, normed_ref, qkv_ref, mixed_ref, second_ref = buffers[:6]
-    query_marks, key_marks, max_columns, sum_columns = work
+    query_marks, key_marks, max_columns, sum_columns, normed_turned, second_turned = work
     rows, width = rows_ref.shape
     head_size = width // HEADS
     per_block = LANES // head_size
@@ -162,6 +172,7 @@
         part = pl.ds(start, LANES)
         hat, _ = normalized(rows_ref[part, :].astype(jnp.float32))
         normed_ref[part, :] = (hat * (1.0 + table[0:1, :]) + table[1:2, :]).astype(jnp.bfloat16)
+    normed_turned[...] = jnp.transpose(normed_ref[...])
     save("normed")
     during("normed", 0)
 
@@ -234,6 +245,7 @@
         part = pl.ds(start, LANES)
         hat, _ = normalized(hidden_ref[part, :])
         second_ref[part, :] = (hat * (1.0 + table[5:6, :]) + table[6:7, :]).astype(jnp.bfloat16)
+    second_turned[...] = jnp.transpose(second_ref[...])
     save("second")
     during("second", 0)
 
@@ -274,14 +286,14 @@
 
 def forward_kernel(block, lengths_ref, rows_ref, tables_ref, *refs):
     own, other, made, (stat_ref,), held, buffers, work, (weight_sems, save_sems) = split_refs(
-        refs, (4, 4, 9, 1, 4, 9, 4, 2)
+        refs, (4, 4, 9, 1, 4, 9, 6, 2)
     )
     weights = Weights((lax.axis_index("section") == block).astype(jnp.int32), own, other, held, weight_sems)
     for index in range(4):
         weights.start(index)
     saves = {
         name: pltpu.make_async_copy(source, target, save_sems.at[index])
-        for index, (name, source, target) in enumerate(zip(SAVED, buffers, made))
+        for index, (name, source, target) in enumerate(zip(SAVED, turned_sources(buffers, work), made))
     }
     table = tables_ref.at[block]
     forward_steps(
@@ -296,12 +308,14 @@
         save.wait()
 
 
-def forward_work(row_count):
+def forward_work(row_count, width):
     return [
         pltpu.VMEM((2, row_count, LANES), jnp.bfloat16),
         pltpu.VMEM((2, row_count, LANES), jnp.bfloat16),
         pltpu.VMEM((row_count, LANES), jnp.float32),
         pltpu.VMEM((row_count, LANES), jnp.float32),
+        pltpu.VMEM((width, row_count), jnp.bfloat16),
+        pltpu.VMEM((width, row_count), jnp.bfloat16),
     ]
 
 
@@ -309,7 +323,7 @@
     return (
         [pltpu.VMEM(w.shape, w.dtype) for w in own]
         + [pltpu.VMEM(s, t) for s, t in kept]
-        + forward_work(row_count)
+        + forward_work(row_count, kept[0][0][1])
         + [pltpu.SemaphoreType.DMA((4,)), pltpu.SemaphoreType.DMA((9,))]
     )
 
@@ -318,32 +332,41 @@
     (
         own, other, (own_down,), made, (stat_ref, other_down), held, buffers, work,
         (own_held, other_held, weight_sems, save_sems, down_sems),
-    ) = split_refs(refs, (3, 3, 1, 7, 2, 3, 8, 4, 5))
+    ) = split_refs(refs, (3, 3, 1, 7, 2, 3, 8, 6, 5))
     section = lax.axis_index("section")
     barrier = pltpu.get_barrier_semaphore()
     pl.semaphore_signal(barrier, inc=1, device_id={"section": 1 - section}, device_id_type=MESH)
     weights = Weights((section == 1).astype(jnp.int32), own, other, held, weight_sems)
     for index in range(3):
         weights.start(index)
-    down = pltpu.make_async_copy(own_down, own_held, down_sems.at[0])
-    down.start()
+    size = own_down.shape[0] // PIECES
+    parts = [pl.ds(piece * size, size) for piece in range(PIECES)]
+    loads = [
+        pltpu.make_async_copy(own_down.at[part], own_held.at[part], down_sems.at[0, piece])
+        for piece, part in enumerate(parts)
+    ]
+    start_copies(loads)
     pl.semaphore_wait(barrier, 1)
-    down.wait()
-    swap = pltpu.make_async_remote_copy(
-        src_ref=own_held, dst_ref=other_held, send_sem=down_sems.at[1], recv_sem=down_sems.at[2],
-        device_id={"section": 1 - section}, device_id_type=MESH,
-    )
-    swap.start()
+    swaps = [
+        pltpu.make_async_remote_copy(
+            src_ref=own_held.at[part], dst_ref=other_held.at[part], send_sem=down_sems.at[1, piece],
+            recv_sem=down_sems.at[2, piece], device_id={"section": 1 - section}, device_id_type=MESH,
+        )
+        for piece, part in enumerate(parts)
+    ]
+    for load, swap in zip(loads, swaps):
+        load.wait()
+        swap.start()
     saves = {
         name: pltpu.make_async_copy(source, target, save_sems.at[index])
-        for index, (name, source, target) in enumerate(zip(SAVED[1:8], buffers[1:], made))
+        for index, (name, source, target) in enumerate(zip(SAVED[1:8], turned_sources(buffers, work)[1:], made))
     }
     forward_steps(
         tables_ref.at[1], lengths_ref, rows_ref, stat_ref, buffers, work, weights.wait,
         lambda name: saves[name].start(), lambda place, i: None,
     )
-    swap.wait()
-    keep = pltpu.make_async_copy(other_held, other_down, down_sems.at[0])
+    wait_copies(swaps)
+    keep = pltpu.make_async_copy(other_held, other_down, down_sems.at[0, 0])
     keep.start()
     up_product(tables_ref.at[1], buffers[5], weights.wait(2), buffers[6], buffers[7])
     saves["slope"].start()
@@ -356,7 +379,7 @@
 def forward_swap(lengths, rows, tables, own, other):
     row_count, width = rows.shape
     kept = saved_shapes(row_count, width, own[2].shape[1])[:8]
-    shapes = kept[1:] + [((16, row_count), jnp.float32), (own[3].shape, own[3].dtype)]
+    shapes = turned_shapes(kept)[1:] + [((16, row_count), jnp.float32), (own[3].shape, own[3].dtype)]
     results = pl.pallas_call(
         forward_swap_kernel,
         out_shape=tuple(jax.ShapeDtypeStruct(s, t) for s, t in shapes),
@@ -364,13 +387,13 @@
         out_specs=[in_place()] * 7 + [in_vmem(), in_place()],
         scratch_shapes=[pltpu.VMEM(w.shape, w.dtype) for w in own[:3]]
         + [pltpu.VMEM(s, t) for s, t in kept]
-        + forward_work(row_count)
+        + forward_work(row_count, width)
         + [
             pltpu.VMEM(own[3].shape, own[3].dtype),
             pltpu.VMEM(own[3].shape, own[3].dtype),
             pltpu.SemaphoreType.DMA((4,)),
             pltpu.SemaphoreType.DMA((9,)),
-            pltpu.SemaphoreType.DMA((3,)),
+            pltpu.SemaphoreType.DMA((3, PIECES)),
         ],
         compiler_params=pltpu.CompilerParams(
             collective_id=2, has_side_effects=True, vmem_limit_bytes=56 * 1024 * 1024
@@ -386,7 +409,7 @@
     stat_shape = (16, row_count)
     return pl.pallas_call(
         functools.partial(forward_kernel, block),
-        out_shape=tuple(jax.ShapeDtypeStruct(s, t) for s, t in kept)
+        out_shape=tuple(jax.ShapeDtypeStruct(s, t) for s, t in turned_shapes(kept))
         + (jax.ShapeDtypeStruct(stat_shape, jnp.float32),),
         in_specs=[in_smem()] + [in_vmem()] * 2 + [in_place()] * 8,
         out_specs=[in_place()] * 9 + [in_vmem()],
@@ -409,14 +432,14 @@
     return groups
 
 
-def opening_kernel(real_shard, lengths_ref, code_tile_ref, vectors_ref, up_bias_ref, patches_ref, book_ref, *refs):
+def opening_kernel(real_shard, lengths_ref, code_tile_ref, vectors_ref, up_bias_ref, patches_ref, book_ref, book_end_ref, *refs):
     (
         own, other, (tables_ref, all_codes_ref, chosen_ref), made, (stat_ref,), held, buffers, work,
         (weight_sems, save_sems),
         (rows_ref, book, total, half_out, half_in, table_in, code_slots, table_out, codes_ref),
         (load_sems, weight_send, weight_got, zero_send, zero_got, middle_send, middle_got, last_send, last_got,
          code_send, code_got, side_send, side_got, keep_sems),
-    ) = split_refs(refs, (3, 3, 3, 7, 1, 3, 8, 4, 2, 9, 14))
+    ) = split_refs(refs, (3, 3, 3, 7, 1, 3, 8, 6, 2, 9, 14))
     section, place = lax.axis_index("section"), lax.axis_index("dp")
     depth = book.shape[2]
     shard_rows, half_width = book.shape[3:]
@@ -436,9 +459,15 @@
         pl.semaphore_signal(barrier, inc=1, device_id={"dp": device}, device_id_type=MESH)
 
     own_book = book.at[my_middle, my_last, my_z]
+    columns = pl.ds(pl.multiple_of(section * half_width, LANES), half_width)
+    whole = shard_rows - book_end_ref.shape[0]
     load_book = pltpu.make_async_copy(
-        book_ref.at[:, pl.ds(pl.multiple_of(section * half_width, LANES), half_width)], own_book, load_sems.at[0]
-    )
+        book_ref.at[pl.ds(0, whole), columns], own_book.at[pl.ds(0, whole)], load_sems.at[0]
+    )
+    load_end = pltpu.make_async_copy(
+        book_end_ref.at[:, columns], own_book.at[pl.ds(whole, shard_rows - whole)], load_sems.at[2]
+    )
+    load_end.start()
     load_book.start()
     load_rows = pltpu.make_async_copy(
         patches_ref.at[pl.ds(pl.multiple_of(section * rows, rows), rows)], rows_ref, load_sems.at[1]
@@ -531,36 +560,47 @@
         return pltpu.make_async_copy(own[index], held[index].at[section], weight_sems.at[index])
 
     def weight_across(index):
-        part = held[index].at[section]
-        return remote(part, part, weight_send.at[index], weight_got.at[index], section=1 - section)
+        copies, size = [], held[index].shape[1] // PIECES
+        for piece in range(PIECES):
+            part = held[index].at[section, pl.ds(piece * size, size)]
+            send, got = weight_send.at[index, piece], weight_got.at[index, piece]
+            copies.append(remote(part, part, send, got, section=1 - section))
+        return copies
+
+    def weight_arrived(index):
+        for copy in weight_across(index):
+            copy.wait_recv()
 
     def keep(index):
         return pltpu.make_async_copy(held[index].at[1 - section], other[index], keep_sems.at[index])
 
     def send_matrix(index):
         own_matrix(index).wait()
-        weight_across(index).start()
+        start_copies(weight_across(index))
 
     table_across = remote(table_out, table_in, side_send.at[0], side_got.at[0], section=1 - section)
     half_across = remote(half_out, half_in, side_send.at[1], side_got.at[1], section=1 - section)
 
+    def pick_rows(which_middle, which_last, block):
+        group = 2 * which_middle + which_last
+        part = pl.ds(pl.multiple_of(block * rows, rows), rows)
+        inside = codes_ref[part, :] - group * GROUP
+        lanes = lax.broadcasted_iota(jnp.int32, (1, depth * shard_rows), 1)
+        hot = jnp.where(inside == lanes, 1.0, 0.0).astype(jnp.bfloat16)
+        shards = book[which_middle, which_last].reshape(depth * shard_rows, half_width)
+        total[part, :] = total[part, :] + times(hot, shards)
+
     def pick(which_middle, which_last):
-        group = 2 * which_middle + which_last
-
         @pl.loop(0, total.shape[0] // rows)
         def _(block):
-            part = pl.ds(pl.multiple_of(block * rows, rows), rows)
-            inside = codes_ref[part, :] - group * GROUP
-            lanes = lax.broadcasted_iota(jnp.int32, (1, depth * shard_rows), 1)
-            hot = jnp.where(inside == lanes, 1.0, 0.0).astype(jnp.bfloat16)
-            shards = book[which_middle, which_last].reshape(depth * shard_rows, half_width)
-            total[part, :] = total[part, :] + times(hot, shards)
+            pick_rows(which_middle, which_last, block)
 
     for index in range(3):
         own_matrix(index).start()
     pl.semaphore_wait(barrier, 3 + depth - 1)
     table_across.start()
     load_book.wait()
+    load_end.wait()
     zero_own(lambda copy: copy.start())
     middle(0).start()
     last(0, 0).start()
@@ -575,7 +615,7 @@
     def weight(index):
         @pl.when(section == 1)
         def _():
-            weight_across(index).wait_recv()
+            weight_arrived(index)
             keep(index).start()
 
         return held[index].at[0]
@@ -583,12 +623,12 @@
     def keep_late(index):
         @pl.when(section == 0)
         def _():
-            weight_across(index).wait_recv()
+            weight_arrived(index)
             keep(index).start()
 
     saves = {
         name: pltpu.make_async_copy(source, target, save_sems.at[index])
-        for index, (name, source, target) in enumerate(zip(SAVED[1:8], buffers[1:], made))
+        for index, (name, source, target) in enumerate(zip(SAVED[1:8], turned_sources(buffers, work)[1:], made))
     }
 
     def from_zero(rank):
@@ -607,10 +647,9 @@
         middle(rank).wait_recv()
         last(1, rank).start()
 
-    def from_last(side):
+    def arrived_last(side):
         for rank in range(depth):
             last(side, rank).wait_recv()
-        pick(my_middle if side == 0 else 1 - my_middle, 1 - my_last)
 
     def during(where, i):
         if where == "normed":
@@ -657,16 +696,19 @@
     up_product(table, buffers[5], weight(2), buffers[6], buffers[7])
     saves["slope"].start()
     saves["act"].start()
-    from_last(0)
+    arrived_last(0)
+    pick(my_middle, 1 - my_last)
     codes_middle().wait_recv()
     codes_last().start()
     keep_late(1)
     keep_late(2)
-    from_last(1)
+    arrived_last(1)
     own_rows = pl.ds(pl.multiple_of(section * rows, rows), rows)
     other_rows = pl.ds(pl.multiple_of((1 - section) * rows, rows), rows)
+    pick_rows(1 - my_middle, 1 - my_last, 1 - section)
     half_out[...] = total[other_rows, :].astype(half_out.dtype)
     half_across.start()
+    pick_rows(1 - my_middle, 1 - my_last, section)
     chosen_ref[:, pl.ds(pl.multiple_of(section * half_width, LANES), half_width)] = total[own_rows, :].astype(
         chosen_ref.dtype
     )
@@ -675,7 +717,8 @@
     codes_last().wait_recv()
     all_codes_ref[...] = code_slots[...]
     for index in range(3):
-        weight_across(index).wait_send()
+        for copy in weight_across(index):
+            copy.wait_send()
         keep(index).wait()
     table_across.wait_send()
     half_across.wait_send()
@@ -703,7 +746,9 @@
     tokens, width = patches.shape
     half_width = width // 2
     depth, shard_rows = devices // 4, codebook.shape[0]
-    padded = jnp.pad(codebook, ((0, -shard_rows % 16), (0, 0)))
+    whole = (shard_rows - 1) // 16 * 16
+    book_end = jnp.pad(codebook[whole:], ((0, -shard_rows % 16), (0, 0)))
+    padded_rows = whole + book_end.shape[0]
     table_shape = (16, width)
     code_tile = codes.reshape(-1, LANES)
     kept = saved_shapes(row_count, width, own[2].shape[1])[:8]
@@ -715,19 +760,19 @@
             ((depth, 2, 2, *code_tile.shape), codes.dtype),
             ((row_count, width), bfloat16),
         ]
-        + kept[1:]
+        + turned_shapes(kept)[1:]
         + [((16, row_count), float32)]
     )
     dma = pltpu.SemaphoreType.DMA
     results = pl.pallas_call(
         functools.partial(opening_kernel, shard_rows),
         out_shape=tuple(jax.ShapeDtypeStruct(s, t) for s, t in shapes),
-        in_specs=[in_smem()] + [in_vmem()] * 3 + [in_place()] * 5,
+        in_specs=[in_smem()] + [in_vmem()] * 3 + [in_place()] * 6,
         out_specs=[in_place()] * 3 + [in_vmem()] * 3 + [in_place()] * 7 + [in_vmem()],
         scratch_shapes=[pltpu.VMEM((2, *w.shape), w.dtype) for w in own[:3]] + forward_scratch((), kept, row_count)
         + [
             pltpu.VMEM((row_count, width), bfloat16),
-            pltpu.VMEM((2, 2, depth, padded.shape[0], half_width), bfloat16),
+            pltpu.VMEM((2, 2, depth, padded_rows, half_width), bfloat16),
             pltpu.VMEM((tokens, half_width), float32),
             pltpu.VMEM((row_count, half_width), bfloat16),
             pltpu.VMEM((row_count, half_width), bfloat16),
@@ -735,9 +780,9 @@
             pltpu.VMEM((depth, 2, 2, *code_tile.shape), codes.dtype),
             pltpu.VMEM(table_shape, float32),
             pltpu.VMEM((tokens, 1), jnp.int32),
-            dma((2,)),
-            dma((4,)),
-            dma((4,)),
+            dma((3,)),
+            dma((3, PIECES)),
+            dma((3, PIECES)),
             dma((depth, depth)),
             dma((depth,)),
             dma((depth,)),
@@ -754,7 +799,7 @@
             collective_id=1, has_side_effects=True, vmem_limit_bytes=60 * 1024 * 1024
         ),
         name="opening",
-    )(lengths, code_tile, vectors, up_bias, patches, padded, *own[:3])
+    )(lengths, code_tile, vectors, up_bias, patches, codebook, book_end, *own[:3])
     return results[:3], results[3], results[4].reshape(devices, -1, LANES), results[5], results[6:]
 
 
@@ -1126,7 +1171,7 @@
     )(lengths, tables, *grads_in, *kept, *own, *other)
 
 
-SLOTS, HELD, RING, LAST_RING = 4, 6, 16, 12
+SLOTS, HELD, RING = 4, 6, 16
 
 
 def chunk_list(width, hidden_units):
@@ -1259,7 +1304,7 @@
         send, got = third_send.at[k, hop - 1], third_got.at[k, hop - 1]
         if k == count:
             return remote(sums_second, sums_third.at[hop - 1], send, got, dp=device)
-        return remote(two.at[k % RING, target], three.at[k % LAST_RING, hop - 1], send, got, dp=device)
+        return remote(two.at[k % RING, target], three.at[k % RING, hop - 1], send, got, dp=device)
 
     def last(k):
         index = k % (count // 2)
@@ -1300,7 +1345,9 @@
                     stage[(k + j) % SLOTS, tile] = product[:, :, j]
 
         else:
-            product = transposed_times(left[...], right[:, j * width : (j + 1) * width]).astype(stage.dtype)
+            columns = right[:, j * width : (j + 1) * width]
+            product = transposed_times(left[...], columns) if operand == 1 else times(left[...], columns)
+            product = product.astype(stage.dtype)
             stage[k % SLOTS] = product.reshape(depth, 2, 2, share, width)
         send_across(k)
         last_of_key = operand == 3 or k + 1 == count or chunks[k + 1][:2] != key
@@ -1361,7 +1408,7 @@
         total = two[slot, my_z].astype(jnp.float32)
         for hop in range(1, depth):
             third(k, hop).wait()
-            total = total + three[k % LAST_RING, hop - 1].astype(jnp.float32)
+            total = total + three[k % RING, hop - 1].astype(jnp.float32)
 
         @pl.when(section == block)
         def _():
@@ -1394,12 +1441,21 @@
         def _():
             last(k).wait_send()
 
-    phases = ((1, begin), (0, give), (3, after_first), (5, after_second), (7, after_third), (8, after_fourth))
+    close = 11
+
+    def times_of(k):
+        start = min(k, count - 1) // 2
+        second_time = max(start + 2, min(start + 3, close + 1))
+        third_time = max(second_time + 1, min(start + 5, close))
+        fourth_time = max(third_time + 1, min(start + 7, close + 1))
+        return start, start + 1, second_time, third_time, fourth_time, fourth_time + 1
+
+    phases = ((1, begin), (0, give), (2, after_first), (3, after_second), (4, after_third), (5, after_fourth))
 
     def step(number):
         for phase, action in phases:
             for k in range(count + 1):
-                if min(k, count - 1) // 2 + phase == number:
+                if times_of(k)[phase] == number:
                     action(k)
 
     mine = pl.ds(pl.multiple_of(section * rows, rows), rows)
@@ -1506,7 +1562,7 @@
         True, lengths_ref, tables_ref.at[0], buffers, enc_sums, enc_weight, enc_arrived, nothing, during_encoder,
     )
     deliver(*grads_enc, True)
-    for number in range(11, (count - 1) // 2 + 9):
+    for number in range(close, times_of(count)[5] + 1):
         step(number)
         if number == 13:
             count_codes_in(codes_ref, code_count, counts_ref, stats_ref)
@@ -1554,10 +1610,10 @@
             pltpu.VMEM((HELD, 2, 2, depth, share, half), bfloat16),
             pltpu.VMEM((RING, 2, depth, share, half), bfloat16),
             pltpu.VMEM((RING, depth, share, half), bfloat16),
-            pltpu.VMEM((LAST_RING, depth - 1, share, half), bfloat16),
+            pltpu.VMEM((RING, depth - 1, share, half), bfloat16),
             pltpu.VMEM((count // 2, share, half), float32),
             pltpu.VMEM((count // 2, share, half), float32),
-            pltpu.VMEM((2, row_count, width), bfloat16),
+            pltpu.VMEM((2, width, row_count), bfloat16),
             pltpu.VMEM((row_count, hidden_units), bfloat16),
             pltpu.VMEM((row_count, width), float32),
             table,
@@ -1583,8 +1639,15 @@
 
 def finish_kernel(vectors_ref, bias_ref, *refs):
     sources, targets, (bias_out, vectors_out), held, (in_sems, out_sems) = split_refs(refs, (6, 6, 2, 6, 2))
-    loads = [pltpu.make_async_copy(s, h, in_sems.at[i]) for i, (s, h) in enumerate(zip(sources, held))]
-    saves = [pltpu.make_async_copy(h, t, out_sems.at[i]) for i, (h, t) in enumerate(zip(held, targets))]
+    pieces = []
+    for source, target, room in zip(sources, targets, held):
+        rows = source.shape[0]
+        step = rows // 4 if rows >= 512 else rows
+        pieces = pieces + [
+            tuple(ref.at[pl.ds(start, step)] for ref in (source, room, target)) for start in range(0, rows, step)
+        ]
+    loads = [pltpu.make_async_copy(s, h, in_sems.at[i]) for i, (s, h, _) in enumerate(pieces)]
+    saves = [pltpu.make_async_copy(h, t, out_sems.at[i]) for i, (_, h, t) in enumerate(pieces)]
     start_copies(loads)
     place = lax.axis_index("dp")
 
@@ -1593,11 +1656,11 @@
         turned = pltpu.roll(ref[...], (whole - place * part) % whole, 1)
         out[...] = turned[: out.shape[0], :part]
 
-    from_place(vectors_ref, vectors_out)
-    from_place(bias_ref, bias_out)
     for load, save in zip(loads, saves):
         load.wait()
         save.start()
+    from_place(vectors_ref, vectors_out)
+    from_place(bias_ref, bias_out)
     wait_copies(saves)
 
 
@@ -1612,7 +1675,7 @@
         in_specs=[in_vmem()] * 2 + [in_place()] * 6,
         out_specs=[in_place()] * 6 + [in_vmem()] * 2,
         scratch_shapes=[pltpu.VMEM(a.shape, a.dtype) for a in results]
-        + [pltpu.SemaphoreType.DMA((6,)), pltpu.SemaphoreType.DMA((6,))],
+        + [pltpu.SemaphoreType.DMA((12,)), pltpu.SemaphoreType.DMA((12,))],
         compiler_params=pltpu.CompilerParams(vmem_limit_bytes=60 * 1024 * 1024),
         name="finish",
     )(vector_sums, bias_sums, *results)
@@ -1650,8 +1713,9 @@
     decoder = ((decoded[1], decoded[3], decoded[4], decoded[6]), (dec_projected, dec_attn, dec_pre, dec_branch))
     results = []
     for index in range(4):
-        enc = transposed_times(encoder[0][index], encoder[1][index])
-        dec = transposed_times(decoder[0][index], decoder[1][index])
+        product = times if index in (0, 2) else transposed_times
+        enc = product(encoder[0][index], encoder[1][index])
+        dec = product(decoder[0][index], decoder[1][index])
         results.append(jnp.where(is_first, enc, dec) + swapped(jnp.where(is_first, dec, enc)))
     own_sums, other_sums = ordered(enc_sums, dec_sums)
     sums = own_sums + swapped(other_sums)

time: 262 us -> 260 us (level)
  no operation moved by 1% of the time
where the time goes in v2:
time: 260 us; the launch traced here: 257 us
  Pallas kernels  254 us (98%)
    pallas_call x1, Pallas kernels, closing(): pl.pallas_call(functools.partial(closing_kernel, chunks, code_count), out...  157 us
    pallas_call x1, Pallas kernels, opening(): pl.pallas_call(functools.partial(opening_kernel, shard_rows), out_shape=t...  62.3 us
    pallas_call x1, Pallas kernels, forward_swap(): pl.pallas_call(forward_swap_kernel, out_shape=tuple((jax.ShapeDtypeStruct...  27.3 us
    pallas_call x1, Pallas kernels, finish(): pl.pallas_call(finish_kernel, out_shape=tuple((jax.ShapeDtypeStruct(a.sha...  6.97 us

profile of v2, /device:TPU:0, one launch (start us, length us, event | category | flops | bytes accessed | tf_op | source)
XLA Modules:
  0.0 257.3 jit_solution(2146148589337717751)
XLA Ops:
  0.6 0.7 slice.6
  1.4 0.6 pad.4.book_end_ref
  2.0 62.3 %opening.1 = (bf16[768,2304]{1,0:T(8,128)(2,1)}, bf16[768,768]{1,0:T(8,128)(2,1)}, bf16[768,3072]{1,0:T(8,128)(2,1)}, f32[2,16,768]{2,1,0:T(8,128)}, s32[4,2,2,8...) custom-call(s32[2,4]{1,0:T(2,128)} %lengths_ref.5, ...), custom_call_target="tpu_custom_call" | custom-call | tf_op jit(solution)/shard_map/opening/pallas_call | solution.py:767
  64.3 27.3 %forward_swap.1 = (f32[512,768]{1,0:T(8,128)}, bf16[768,512]{1,0:T(8,128)(2,1)}, bf16[512,2304]{1,0:T(8,128)(2,1)}, bf16[512,768]{1,0:T(8,128)(2,1)}, bf16[768,5...) custom-call(s32[2,4]{1,0:T(2,128)} %lengths_ref.5, ...), custom_call_target="tpu_custom_call" | custom-call | tf_op jit(solution)/shard_map/forward_swap/pallas_call | solution.py:383
  91.6 157.3 %closing.1 = (f32[48,2304]{1,0:T(8,128)}, f32[48,768]{1,0:T(8,128)}, f32[48,3072]{1,0:T(8,128)}, f32[192,768]{1,0:T(8,128)}, f32[8,768]{1,0:T(8,128)}, /*index=5...) custom-call(s32[2,4]{1,0:T(2,128)} %lengths_ref.5, ...), custom_call_target="tpu_custom_call" | custom-call | tf_op jit(solution)/shard_map/closing/pallas_call | solution.py:1599
  248.9 0.0 copy-start
  248.9 0.0 copy-start.1
  249.0 7.0 %finish.1 = (f32[48,2304]{1,0:T(8,128)}, f32[48,768]{1,0:T(8,128)}, f32[48,3072]{1,0:T(8,128)}, f32[192,768]{1,0:T(8,128)}, bf16[1024,768]{1,0:T(8,128)(2,1)}, /...) custom-call(f32[8,768]{1,0:T(8,128)} %get-tuple-element.74.vectors_ref, ...), custom_call_target="tpu_custom_call" | custom-call | tf_op jit(solution)/shard_map/finish/pallas_call | solution.py:1672
  255.9 0.0 copy-done
  255.9 0.6 copy.23
  256.6 0.0 copy-done.1
  256.6 0.5 copy.24
Async XLA Ops:
  248.9 7.0 %copy-start = (s32[50,128]{1,0:T(8,128)S(1)}, s32[50,128]{1,0:T(8,128)}, u32[]{:S(2)}) copy-start(s32[50,128]{1,0:T(8,128)} %get-tuple-element.90) | copy-start | bytes 76804
  248.9 7.6 %copy-start.1 = (f32[1,2]{1,0:T(1,128)S(1)}, f32[1,2]{1,0:T(1,128)}, u32[]{:S(2)}) copy-start(f32[1,2]{1,0:T(1,128)} %get-tuple-element.91) | copy-start | bytes 28

commit v3 on v2

--- a/solution.py
+++ b/solution.py
@@ -1445,10 +1445,7 @@
 
     def times_of(k):
         start = min(k, count - 1) // 2
-        second_time = max(start + 2, min(start + 3, close + 1))
-        third_time = max(second_time + 1, min(start + 5, close))
-        fourth_time = max(third_time + 1, min(start + 7, close + 1))
-        return start, start + 1, second_time, third_time, fourth_time, fourth_time + 1
+        return tuple(start + stage_number for stage_number in range(6))
 
     phases = ((1, begin), (0, give), (2, after_first), (3, after_second), (4, after_third), (5, after_fourth))
 

time: 260 us -> 257 us (0.988)
  Pallas kernels: 254 us -> 251 us
    pallas_call x1, Pallas kernels: 157 us -> 154 us  [closing(): pl.pallas_call(functools.partial(closing_kernel, chunks, code_count), out...]
where the time goes in v3:
time: 257 us; the launch traced here: 254 us
  Pallas kernels  251 us (98%)
    pallas_call x1, Pallas kernels, closing(): pl.pallas_call(functools.partial(closing_kernel, chunks, code_count), out...  154 us
    pallas_call x1, Pallas kernels, opening(): pl.pallas_call(functools.partial(opening_kernel, shard_rows), out_shape=t...  62.3 us
    pallas_call x1, Pallas kernels, forward_swap(): pl.pallas_call(forward_swap_kernel, out_shape=tuple((jax.ShapeDtypeStruct...  27.3 us
    pallas_call x1, Pallas kernels, finish(): pl.pallas_call(finish_kernel, out_shape=tuple((jax.ShapeDtypeStruct(a.sha...  6.97 us

profile of v3, /device:TPU:0, one launch (start us, length us, event | category | flops | bytes accessed | tf_op | source)
XLA Modules:
  0.0 254.1 jit_solution(9244008984054280401)
XLA Ops:
  0.6 0.7 slice.6
  1.4 0.6 pad.4.book_end_ref
  2.0 62.3 %opening.1 = (bf16[768,2304]{1,0:T(8,128)(2,1)}, bf16[768,768]{1,0:T(8,128)(2,1)}, bf16[768,3072]{1,0:T(8,128)(2,1)}, f32[2,16,768]{2,1,0:T(8,128)}, s32[4,2,2,8...) custom-call(s32[2,4]{1,0:T(2,128)} %lengths_ref.5, ...), custom_call_target="tpu_custom_call" | custom-call | tf_op jit(solution)/shard_map/opening/pallas_call | solution.py:767
  64.3 27.3 %forward_swap.1 = (f32[512,768]{1,0:T(8,128)}, bf16[768,512]{1,0:T(8,128)(2,1)}, bf16[512,2304]{1,0:T(8,128)(2,1)}, bf16[512,768]{1,0:T(8,128)(2,1)}, bf16[768,5...) custom-call(s32[2,4]{1,0:T(2,128)} %lengths_ref.5, ...), custom_call_target="tpu_custom_call" | custom-call | tf_op jit(solution)/shard_map/forward_swap/pallas_call | solution.py:383
  91.6 154.1 %closing.1 = (f32[48,2304]{1,0:T(8,128)}, f32[48,768]{1,0:T(8,128)}, f32[48,3072]{1,0:T(8,128)}, f32[192,768]{1,0:T(8,128)}, f32[8,768]{1,0:T(8,128)}, /*index=5...) custom-call(s32[2,4]{1,0:T(2,128)} %lengths_ref.5, ...), custom_call_target="tpu_custom_call" | custom-call | tf_op jit(solution)/shard_map/closing/pallas_call | solution.py:1596
  245.7 0.0 copy-start
  245.7 0.0 copy-start.1
  245.8 7.0 %finish.1 = (f32[48,2304]{1,0:T(8,128)}, f32[48,768]{1,0:T(8,128)}, f32[48,3072]{1,0:T(8,128)}, f32[192,768]{1,0:T(8,128)}, bf16[1024,768]{1,0:T(8,128)(2,1)}, /...) custom-call(f32[8,768]{1,0:T(8,128)} %get-tuple-element.74.vectors_ref, ...), custom_call_target="tpu_custom_call" | custom-call | tf_op jit(solution)/shard_map/finish/pallas_call | solution.py:1669
  252.7 0.0 copy-done
  252.7 0.6 copy.23
  253.4 0.0 copy-done.1
  253.4 0.5 copy.24
Async XLA Ops:
  245.7 7.0 %copy-start = (s32[50,128]{1,0:T(8,128)S(1)}, s32[50,128]{1,0:T(8,128)}, u32[]{:S(2)}) copy-start(s32[50,128]{1,0:T(8,128)} %get-tuple-element.90) | copy-start | bytes 76804
  245.7 7.6 %copy-start.1 = (f32[1,2]{1,0:T(1,128)S(1)}, f32[1,2]{1,0:T(1,128)}, u32[]{:S(2)}) copy-start(f32[1,2]{1,0:T(1,128)} %get-tuple-element.91) | copy-start | bytes 28
